TPU v7x, 32 devices: a whole 2x2x4 slice. The times are simulated.
32 devices in a mesh: seq: 16 (over z, y, core), head: 2 (over x).
Axes of the slice: x: 2, y: 2, z: 4, core: 2. Of those that a mesh axis runs over, the one named last changes fastest.
Arguments:
- query_rows: bfloat16 [5120, 3072], P('seq', 'head'), may hold values from -6 to 6
- key_rows: bfloat16 [5120, 3072], P('seq', 'head'), may hold values from -6 to 6
- value_rows: bfloat16 [5120, 3072], P('seq', 'head'), may hold values from -6 to 6
- pattern: int32 [16, 6], P('seq'), may hold values 0 or 1
- owners: int32 [4], replicated, may hold values from 0 to 15, as said below
- out_weight: bfloat16 [3072, 3072], P('head'), may hold values from -0.15625 to 0.15625
Outputs:
- mixed: bfloat16 [5120, 3072], P('seq', 'head')
Inputs may be any that keep to these rules, and one draw needn't show every extreme that they name: `owners`: distinct block indices; blocks 0 and 16 - 1 are always among them.
All inputs are finite; a program needn't handle non-finite values. No bound on the sum of `pattern` on one device may be relied on, other than what follows from the above.
Results may differ from a plain program's by a relative error of at most 0.02.
Values may be sent and summed in bfloat16 or wider, within the bound.
No kernel may reach another device: no remote copies, remote signals or barrier semaphores. Data moves between devices by JAX's collectives and lax.ppermute only.
A program may use at most 128 MiB of HBM per device.

v0:
```python
import functools

import jax
import jax.numpy as jnp
from jax import lax
from jax.experimental import pallas as pl
from jax.experimental.pallas import tpu as pltpu
from jax.sharding import PartitionSpec as P

HD = 128
REACH = 3
OWNERS = 4
REF_DEV = 256
GROUP = 4
PLANES = 4
CHUNKS = (2, 1)
PAT_ROWS = 16
NEG = -1e30
LOG2E = 1.4426950408889634
F32 = jnp.float32
BF16 = jnp.bfloat16


def broadcast(block, axis, owner):
    block = jnp.where(lax.axis_index(axis) == owner, block, jnp.zeros_like(block))
    return lax.psum(block, axis)


def from_behind(value, axis, steps):
    count = lax.axis_size(axis)
    pairs = [(source, (source + steps) % count) for source in range(count)]
    return lax.ppermute(value, axis, pairs)


def column_of(offset):
    return offset + REACH if offset < 0 else offset + REACH - 1


def merge_block(state, query_three, block_keys, block_values):
    peaks, totals, summed_values = state
    local_heads = query_three.shape[1]
    keys_three = block_keys.reshape(-1, local_heads, HD)
    values_three = block_values.reshape(-1, local_heads, HD)
    scores = jnp.einsum(
        "qhd,khd->hqk", query_three, keys_three, preferred_element_type=jnp.float32
    ) * HD ** (-0.5)
    new_peaks = jnp.maximum(peaks, jnp.max(scores, axis=-1))
    rescale = jnp.exp(peaks - new_peaks)
    weights = jnp.exp(scores - new_peaks[:, :, None])
    totals = totals * rescale + jnp.sum(weights, axis=-1)
    contrib = jnp.einsum(
        "hqk,khd->hqd",
        weights.astype(jnp.bfloat16),
        values_three,
        preferred_element_type=jnp.float32,
    )
    summed_values = summed_values * rescale[:, :, None] + contrib
    return (new_peaks, totals, summed_values)


def absorb(state, query_three, stacked, active):
    return lax.cond(
        active,
        lambda inner: merge_block(inner, query_three, stacked[0], stacked[1]),
        lambda inner: inner,
        state,
    )


def plain_body(query_rows, key_rows, value_rows, pattern, owners, out_weight):
    row_count = query_rows.shape[0]
    local_width = query_rows.shape[1]
    local_heads = local_width // HD
    query_three = query_rows.reshape(row_count, local_heads, HD)
    start_state = (
        jnp.full((local_heads, row_count), -jnp.inf, jnp.float32),
        jnp.zeros((local_heads, row_count), jnp.float32),
        jnp.zeros((local_heads, row_count, HD), jnp.float32),
    )
    state = merge_block(start_state, query_three, key_rows, value_rows)
    own_stack = jnp.stack([key_rows, value_rows])
    ref_stack = jnp.stack([key_rows[:REF_DEV], value_rows[:REF_DEV]])
    for member in range(OWNERS):
        arrived = broadcast(ref_stack, "seq", owners[member])
        state = merge_block(state, query_three, arrived[0], arrived[1])
    for distance in range(1, REACH + 1):
        for offset in (-distance, distance):
            arrived = from_behind(own_stack, "seq", -offset)
            state = absorb(state, query_three, arrived, pattern[0, column_of(offset)] != 0)
    peaks, totals, summed_values = state
    attended = summed_values / totals[:, :, None]
    attended = (
        jnp.transpose(attended, (1, 0, 2)).reshape(row_count, local_width).astype(jnp.bfloat16)
    )
    partial_value = jnp.dot(attended, out_weight, preferred_element_type=jnp.float32)
    return lax.psum_scatter(
        partial_value.astype(jnp.bfloat16), "head", scatter_dimension=1, tiled=True
    )


def attend_kernel(heads, plan, first, last, flags_ref, *refs):
    slots = sum(plan)
    q_in = refs[:GROUP]
    ins = refs[GROUP : GROUP + len(plan)]
    rest = refs[GROUP + len(plan) :]
    if not first:
        state_in, rest = rest[:3], rest[3:]
    outs, rest = rest[: GROUP if last else 3], rest[GROUP if last else 3 :]
    q_buf, kv_buf, vt_buf, todo, peak, total, acc, q_sem, kv_sem, state_sem = rest
    rows = q_buf.shape[1]
    width = heads * HD
    scale = HD**-0.5 * LOG2E
    copies = [
        pltpu.make_async_copy(q_in[m].at[2, pl.ds(0, rows)], q_buf.at[m], q_sem.at[m])
        for m in range(GROUP)
    ]
    if first:
        peak[...] = jnp.full(peak.shape, NEG, F32)
        total[...] = jnp.zeros(total.shape, F32)
        acc[...] = jnp.zeros(acc.shape, F32)
    else:
        for n, buf in enumerate((peak, total, acc)):
            copies.append(pltpu.make_async_copy(state_in[n], buf, state_sem.at[n]))
    slot = 0
    for ref, count in zip(ins, plan):
        for j in range(count):
            copies.append(pltpu.make_async_copy(ref.at[j], kv_buf.at[slot], kv_sem.at[slot]))
            slot += 1
    for copy in copies:
        copy.start()

    counts = []
    for m in range(GROUP):

        def note(s, at):
            todo[m, at] = s
            return at + jnp.where(flags_ref[m, s] > 0, 1, 0)

        count = lax.fori_loop(0, slots, note, 0)
        todo[m, count] = -1
        counts.append(count)
    for copy in copies:
        copy.wait()

    def turn(s, _):
        for h in range(heads):
            vt_buf[s, h] = kv_buf[s, 1, :, pl.ds(h * HD, HD)].T
        return 0

    lax.fori_loop(0, slots, turn, 0)
    ends = (0, REF_DEV, rows)

    def one_query(m):
        def pair(p, _):
            chosen = []
            for e in range(2):
                s = todo[m, 2 * p + e]
                shut = s < 0
                s = jnp.maximum(s, 0)
                flag = jnp.where(shut, 0, flags_ref[m, s])
                some = jnp.where(flag == 3, 1.0, jnp.where(flag == 0, NEG, 0.0))
                other = jnp.where((flag & 1) == 1, 0.0, NEG)
                chosen.append((s, (some, other)))
            for h in range(heads):
                cols = pl.ds(h * HD, HD)
                q = q_buf[m, :, cols]
                new = peak[m, h]
                scores = []
                for s, bias in chosen:
                    for part in range(2):
                        k = kv_buf[s, 0, pl.ds(ends[part], ends[part + 1] - ends[part]), cols]
                        raw = (
                            lax.dot_general(
                                k, q, (((1,), (1,)), ((), ())), preferred_element_type=F32
                            )
                            * scale
                        )
                        new = jnp.maximum(new, jnp.max(raw, axis=0, keepdims=True) + bias[part])
                        scores.append((raw, bias[part]))
                keep = jnp.exp2(peak[m, h] - new)
                sums = total[m, h] * keep
                out = acc[m, h] * keep
                for e, (s, _) in enumerate(chosen):
                    weights = []
                    for raw, bias in scores[2 * e : 2 * e + 2]:
                        weight = jnp.exp2(raw - (new - bias))
                        sums = sums + jnp.sum(weight, axis=0, keepdims=True)
                        weights.append(weight.astype(BF16))
                    out = out + jnp.dot(
                        vt_buf[s, h], jnp.concatenate(weights, axis=0), preferred_element_type=F32
                    )
                peak[m, h] = new
                total[m, h] = sums
                acc[m, h] = out
            return 0

        lax.fori_loop(0, (counts[m] + 1) // 2, pair, 0)

    for m in range(GROUP):
        one_query(m)
    if last:
        for m in range(GROUP):
            for h in range(heads):
                outs[m][:, pl.ds(h * HD, HD)] = (acc[m, h] / total[m, h]).T.astype(BF16)
    else:
        for out, buf in zip(outs, (peak, total, acc)):
            out[...] = buf[...]


def attend(flags, own, held, state, last):
    rows, width = held[0].shape[2:]
    heads = width // HD
    plan = tuple(array.shape[0] for array in held)
    slots = sum(plan)
    any_spec = pl.BlockSpec(memory_space=pl.ANY)
    vmem_spec = pl.BlockSpec(memory_space=pltpu.VMEM)
    state_shapes = [(GROUP, heads, 1, rows)] * 2 + [(GROUP, heads, HD, rows)]
    if last:
        out_shape = [jax.ShapeDtypeStruct((rows, width), BF16)] * GROUP
    else:
        out_shape = [jax.ShapeDtypeStruct(shape, F32) for shape in state_shapes]
    state = state or []
    return pl.pallas_call(
        functools.partial(attend_kernel, heads, plan, not state, last),
        out_shape=out_shape,
        in_specs=[pl.BlockSpec(memory_space=pltpu.SMEM)]
        + [any_spec] * (GROUP + len(held) + len(state)),
        out_specs=[vmem_spec] * len(out_shape),
        scratch_shapes=[
            pltpu.VMEM((GROUP, rows, width), BF16),
            pltpu.VMEM((slots, 2, rows, width), BF16),
            pltpu.VMEM((slots, heads, HD, rows), BF16),
            pltpu.SMEM((GROUP, slots + 2), jnp.int32),
        ]
        + [pltpu.VMEM(shape, F32) for shape in state_shapes]
        + [
            pltpu.SemaphoreType.DMA((GROUP,)),
            pltpu.SemaphoreType.DMA((slots,)),
            pltpu.SemaphoreType.DMA((3,)),
        ],
        compiler_params=pltpu.CompilerParams(vmem_limit_bytes=48 << 20),
        cost_estimate=pl.CostEstimate(flops=0, bytes_accessed=0, transcendentals=0),
        name="attend_slots",
    )(flags, *own, *held, *state)


def grouped_body(query_rows, key_rows, value_rows, pattern, owners, out_weight):
    rows, width = query_rows.shape
    out_cols = out_weight.shape[1] // 2
    blocks = GROUP * PLANES
    index = lax.axis_index("seq")
    side = lax.axis_index("head")
    plane, member = index // GROUP, index % GROUP
    per_plane = width // HD // PLANES
    chunks = CHUNKS if sum(CHUNKS) == per_plane else (per_plane,)
    starts = [sum(chunks[:c]) for c in range(len(chunks))]

    def swap(value, bits):
        return lax.ppermute(value, "seq", [(i, i ^ bits) for i in range(blocks)])

    def swap_planes(value, k):
        return swap(value, GROUP * k)

    def across(value):
        return lax.ppermute(value, "head", [(0, 1), (1, 0)])

    def after(value, *others):
        return lax.optimization_barrier((value, others))[0]

    def pack_heads(arrays, start, heads):
        note = jnp.pad(
            (pattern != 0).astype(BF16)[None],
            ((0, 2), (rows, PAT_ROWS - 1), (0, heads * HD - 2 * REACH)),
        )
        pieces = []
        for k in range(PLANES):
            first = ((plane ^ k) * per_plane + start) * HD
            piece = jnp.stack(
                [lax.dynamic_slice_in_dim(array, first, heads * HD, 1) for array in arrays]
            )
            pieces.append(jnp.pad(piece, ((0, 0), (0, PAT_ROWS), (0, 0))) + note)
        return pieces

    arrays = (key_rows, value_rows, query_rows)
    half = width // 2
    core = index % 2
    packed = [pack_heads(arrays, starts[0], chunks[0])]
    weight = after(out_weight, packed[0])
    theirs = lax.dynamic_slice(weight, (core * half, (1 - side) * out_cols), (half, out_cols))
    part = across(theirs)
    for c in range(1, len(chunks)):
        arrays = after(arrays, packed[-1], theirs)
        packed.append(pack_heads(arrays, starts[c], chunks[c]))

    pieces_all, shared = [], []
    for c in range(len(chunks)):
        pieces = packed[c]
        if c > 0:
            before = pieces_all[-1]
            pieces = [
                pieces[0],
                after(pieces[1], before[3]),
                after(pieces[2], before[2]),
                after(pieces[3], before[1]),
            ]
        pieces = [pieces[0]] + [swap_planes(pieces[k], k) for k in range(1, PLANES)]
        mine = jnp.stack([piece[:2, :rows] for piece in pieces])
        beside = swap(mine, 1)
        chip = swap(mine, 2)
        chip_beside = swap(chip, 1)
        pieces_all.append(pieces)
        shared.append((mine, beside, chip, chip_beside))

    planes_at = (plane ^ jnp.arange(PLANES, dtype=jnp.int32)) * GROUP
    my_blocks = planes_at + member
    held = jnp.concatenate([planes_at + (member ^ m) for m in range(GROUP)])
    my_pattern = jnp.stack([piece[0, rows, : 2 * REACH] for piece in pieces_all[0]])
    away = (held[None, :] - my_blocks[:, None]) % blocks
    full = (away == 0).astype(jnp.int32)
    for offset in list(range(-REACH, 0)) + list(range(1, REACH + 1)):
        chosen = (my_pattern[:, column_of(offset)] != 0)[:, None]
        full = full + (chosen & (away == offset % blocks)).astype(jnp.int32)
    is_ref = jnp.any(held[:, None] == owners[None, :], axis=1).astype(jnp.int32)
    flags = full + 2 * is_ref[None, :]
    near_flags, far_flags = flags[:, : 2 * PLANES], flags[:, 2 * PLANES :]

    def weight_rows(weight, start, heads):
        return jnp.concatenate(
            [
                lax.dynamic_slice_in_dim(
                    weight, ((plane ^ k) * per_plane + start) * HD, heads * HD, 0
                )
                for k in range(PLANES)
            ]
        )

    mixed = jnp.zeros((rows, out_cols), F32)
    weights = []
    done = []
    for c in range(len(chunks)):
        own = pieces_all[c]
        mine, beside, chip, chip_beside = shared[c]
        if c > 0:
            own = after(own, done[-1])
        state = attend(near_flags, own, [mine, beside], None, False)
        if c == 0:
            part = after(part, state)
            rest = swap(part, 1)
            weight_far = jnp.where(
                core == 0, jnp.concatenate([part, rest]), jnp.concatenate([rest, part])
            )
            weight_near = lax.dynamic_slice_in_dim(out_weight, side * out_cols, out_cols, 1)
            weights = [
                [weight_rows(weight, starts[n], chunks[n]) for weight in (weight_near, weight_far)]
                for n in range(len(chunks))
            ]
        else:
            state = after(state, weights)
        outs = attend(far_flags, own, [chip, chip_beside], list(state), True)
        done.append(outs)
        near = jnp.concatenate(
            [outs[0]] + [swap_planes(outs[k], k) for k in range(1, PLANES)], axis=1
        )
        far = across(near)
        weight_n, weight_f = weights[c]
        mixed = mixed + jnp.dot(near, weight_n, preferred_element_type=F32)
        mixed = mixed + jnp.dot(far, weight_f, preferred_element_type=F32)
    return mixed.astype(BF16)


def body(query_rows, key_rows, value_rows, pattern, owners, out_weight):
    fits = (
        lax.axis_size("seq") == GROUP * PLANES
        and lax.axis_size("head") == 2
        and (query_rows.shape[1] // HD) % PLANES == 0
    )
    plan = grouped_body if fits else plain_body
    return plan(query_rows, key_rows, value_rows, pattern, owners, out_weight)


def solution(mesh):
    return jax.shard_map(
        body,
        mesh=mesh,
        in_specs=(
            P("seq", "head"),
            P("seq", "head"),
            P("seq", "head"),
            P("seq", None),
            P(),
            P("head", None),
        ),
        out_specs=P("seq", "head"),
        check_vma=False,
    )
```

profile of v0, /device:TPU:0, one launch (start us, length us, event | category | flops | bytes accessed | tf_op | source)
XLA Modules:
  0.0 170.7 jit_solution(4142732279225175985)
XLA Ops:
  4.3 5.0 %collective-permute-start.2 = (bf16[3,336,256]{2,1,0:T(8,128)(2,1)}, bf16[3,336,256]{2,1,0:T(8,128)(2,1)S(1)}, u32[]{:S(2)}, u32[]{:S(2)}) collective-permute-start(bf16[3,336,256]{2,1,0:T(8,128)(2,1)} %get-tuple-element.118), channel_id=1, source_target_pairs={{0,24},{2,26},{4,28},{6,30},{8,16},{10,18},{12,20},{14,22},{16,8},... | collective-permute-start | bytes 1548296 | tf_op jit(solution)/shard_map/ppermute | solution.py:259
  9.9 3.3 %dynamic_slice.140 = bf16[768,1536]{1,0:T(8,128)(2,1)} dynamic-slice(bf16[1536,3072]{1,0:T(8,128)(2,1)} %param.11, s32[]{:T(128)S(6)} %select_n.127, s32[]{:T(128)S(6)} %select_n.128), dynamic_slice_sizes={768,1536} | dynamic-slice | bytes 4718596 | tf_op jit(solution)/shard_map/dynamic_slice | solution.py:289
  13.2 1.7 %collective-permute-start.10 = (bf16[768,1536]{1,0:T(8,128)(2,1)}, bf16[768,1536]{1,0:T(8,128)(2,1)}, u32[]{:S(2)}, u32[]{:S(2)}) collective-permute-start(bf16[768,1536]{1,0:T(8,128)(2,1)} %dynamic_slice.140), channel_id=1, source_target_pairs={{0,1},{1,0},{2,3},{3,2},{4,5},{5,4},{6,7},{7,6},{8,9},{9,8},{10,11... | collective-permute-start | bytes 7077896 | tf_op jit(solution)/shard_map/ppermute | solution.py:265
  19.2 3.1 %collective-permute-done.2.refs_3_ = bf16[3,336,256]{2,1,0:T(8,128)(2,1)S(1)} collective-permute-done((bf16[3,336,256]{2,1,0:T(8,128)(2,1)}, bf16[3,336,256]{2,1,0:T(8,128)(2,1)S(1)}, u32[]{:S(2)}, u32[]{:S(2)}) %collective-permute-start.2) | collective-permute-done | bytes 516128 | tf_op jit(solution)/shard_map/ppermute | solution.py:259
  22.3 31.3 %collective-permute-done.1.refs_2_ = bf16[3,336,256]{2,1,0:T(8,128)(2,1)S(1)} collective-permute-done((bf16[3,336,256]{2,1,0:T(8,128)(2,1)S(1)}, bf16[3,336,256]{2,1,0:T(8,128)(2,1)S(1)}, u32[]{:S(2)}, u32[]{:S(2)}) %collective-permute-start.1) | collective-permute-done | bytes 516128 | tf_op jit(solution)/shard_map/ppermute | solution.py:259
  53.9 1.6 collective-permute-start.3
  55.5 2.5 %collective-permute-start.14 = (bf16[3,336,128]{2,1,0:T(8,128)(2,1)}, bf16[3,336,128]{2,1,0:T(8,128)(2,1)}, u32[]{:S(2)}, u32[]{:S(2)}) collective-permute-start(bf16[3,336,128]{2,1,0:T(8,128)(2,1)} %get-tuple-element.48), channel_id=1, source_target_pairs={{0,24},{2,26},{4,28},{6,30},{8,16},{10,18},{12,20},{14,22},{16,8},... | collective-permute-start | bytes 774152 | tf_op jit(solution)/shard_map/ppermute | solution.py:259
  58.5 15.3 %attend_slots.4 = (f32[4,2,1,320]{3,2,1,0:T(1,128)S(1)}, f32[4,2,1,320]{3,2,1,0:T(1,128)S(1)}, f32[4,2,128,320]{3,2,1,0:T(8,128)}) custom-call(s32[4,8]{1,0:T(4,128)S(1)} %get-tuple-element.109.flags_ref, bf16[3,336,256]{2,1,0:T(8,128)(2,1)S(1)} %get-tuple-element.115.refs_0_, bf16[3,336,256]{2,1,0:T(8,128)(2,1)S(1)} %collective-permute-done.refs_1_, ...), custom_call_target="tpu_custom_call" | custom-call | tf_op jit(solution)/shard_map/attend_slots/pallas_call | solution.py:223
  76.1 1.6 collective-permute-start.12
  77.7 6.2 %collective-permute-done.3.refs_4_ = bf16[4,2,320,256]{3,2,1,0:T(8,128)(2,1)} collective-permute-done((bf16[4,2,320,256]{3,2,1,0:T(8,128)(2,1)S(1)}, bf16[4,2,320,256]{3,2,1,0:T(8,128)(2,1)}, u32[]{:S(2)}, u32[]{:S(2)}) %collective-permute-start.3) | collective-permute-done | bytes 1310752 | tf_op jit(solution)/shard_map/ppermute | solution.py:259
  87.5 1.6 collective-permute-start.15
  89.1 5.4 %fusion.45 = (bf16[256,1536]{1,0:T(8,128)(2,1)}, bf16[256,1536]{1,0:T(8,128)(2,1)}, bf16[256,1536]{1,0:T(8,128)(2,1)}, bf16[256,1536]{1,0:T(8,128)(2,1)}) fusion(bf16[1536,3072]{1,0:T(8,128)(2,1)} %param.11, s32[]{:T(128)S(6)} %select_n.119, s32[]{:T(128)S(6)} %select_n.121, s32[]{:T(128)S(6)} %select_n.124, s32[]{:T(128)S(6)} %select_n.123, s32[]{:T(128)S(6)} %select_n.122), kind=kLoop, calls=%fused_computation.137 | loop fusion | bytes 6291476 | tf_op jit(solution)/shard_map/dynamic_slice | solution.py:330
  94.8 2.3 %fusion.46 = (bf16[128,1536]{1,0:T(8,128)(2,1)S(1)}, bf16[128,1536]{1,0:T(8,128)(2,1)S(1)}, bf16[128,1536]{1,0:T(8,128)(2,1)S(1)}, bf16[128,1536]{1,0:T(8,128)(2,1)S(1)}) fusion(bf16[1536,3072]{1,0:T(8,128)(2,1)} %param.11, s32[]{:T(128)S(6)} %select_n.134, s32[]{:T(128)S(6)} %select_n.121, s32[]{:T(128)S(6)} %select_n.135, s32[]{:T(128)S(6)} %select_n.137, ...), kind=kLoop, calls=%fused_computation.138 | loop fusion | bytes 3145748 | tf_op jit(solution)/shard_map/dynamic_slice | solution.py:330
  97.1 13.3 %attend_slots.5 = (bf16[320,256]{1,0:T(8,128)(2,1)S(1)}, bf16[320,256]{1,0:T(8,128)(2,1)}, bf16[320,256]{1,0:T(8,128)(2,1)S(1)}, bf16[320,256]{1,0:T(8,128)(2,1)S(1)}) custom-call(s32[4,8]{1,0:T(4,128)S(1)} %get-tuple-element.110.flags_ref, bf16[3,336,256]{2,1,0:T(8,128)(2,1)S(1)} %get-tuple-element.115.refs_0_, ...), custom_call_target="tpu_custom_call" | custom-call | tf_op jit(solution)/shard_map/attend_slots/pallas_call | solution.py:223
  113.2 2.9 %collective-permute-start.16 = (bf16[4,2,320,128]{3,2,1,0:T(8,128)(2,1)S(1)}, bf16[4,2,320,128]{3,2,1,0:T(8,128)(2,1)S(1)}, u32[]{:S(2)}, u32[]{:S(2)}) collective-permute-start(bf16[4,2,320,128]{3,2,1,0:T(8,128)(2,1)S(1)} %collective-permute-done.15.refs_4_), channel_id=1, source_target_pairs={{0,2},{2,0},{4,6},{6,4},{8,10},{10,8},{12,14},{14,12},{16,18},{18,... | collective-permute-start | bytes 1966088 | tf_op jit(solution)/shard_map/ppermute | solution.py:259
  116.1 2.6 %collective-permute-start.7 = (bf16[320,256]{1,0:T(8,128)(2,1)S(1)}, bf16[320,256]{1,0:T(8,128)(2,1)S(1)}, u32[]{:S(2)}, u32[]{:S(2)}) collective-permute-start(bf16[320,256]{1,0:T(8,128)(2,1)S(1)} %copy-done.11), channel_id=1, source_target_pairs={{0,16},{2,18},{4,20},{6,22},{8,24},{10,26},{12,28},{14,30},{16,0},... | collective-permute-start | bytes 491528 | tf_op jit(solution)/shard_map/ppermute | solution.py:259
  118.7 1.6 collective-permute-start.8
  120.3 9.5 %attend_slots.6 = (f32[4,1,1,320]{3,2,1,0:T(1,128)S(1)}, f32[4,1,1,320]{3,2,1,0:T(1,128)S(1)}, f32[4,1,128,320]{3,2,1,0:T(8,128)S(1)}) custom-call(s32[4,8]{1,0:T(4,128)S(1)} %get-tuple-element.109.flags_ref, bf16[3,336,128]{2,1,0:T(8,128)(2,1)S(1)} %copy-done.1, bf16[3,336,128]{2,1,0:T(8,128)(2,1)S(1)} %copy-done.3, ...), custom_call_target="tpu_custom_call" | custom-call | tf_op jit(solution)/shard_map/attend_slots/pallas_call | solution.py:223
  132.5 5.0 %maximum_select_fusion = bf16[1536,1536]{1,0:T(8,128)(2,1)S(1)} fusion(bf16[768,1536]{1,0:T(8,128)(2,1)} %collective-permute-done.11, bf16[768,1536]{1,0:T(8,128)(2,1)} %collective-permute-done.10, pred[]{:T(512)S(6)} %eq.74), kind=kLoop, calls=%fused_computation | loop fusion | flops 21233664 | bytes 9437185 | tf_op jit(solution)/shard_map/jit(_where)/select_n | solution.py:349
  138.2 8.4 %attend_slots.7 = (bf16[320,128]{1,0:T(8,128)(2,1)S(1)}, bf16[320,128]{1,0:T(8,128)(2,1)S(1)}, bf16[320,128]{1,0:T(8,128)(2,1)S(1)}, bf16[320,128]{1,0:T(8,128)(2,1)S(1)}) custom-call(s32[4,8]{1,0:T(4,128)S(1)} %get-tuple-element.110.flags_ref, bf16[3,336,128]{2,1,0:T(8,128)(2,1)S(1)} %copy-done.1, bf16[3,336,128]{2,1,0:T(8,128)(2,1)S(1)} %copy-done.3, ...), custom_call_target="tpu_custom_call" | custom-call | tf_op jit(solution)/shard_map/attend_slots/pallas_call | solution.py:223
  146.7 3.2 %collective-permute-start.18 = (bf16[320,128]{1,0:T(8,128)(2,1)S(1)}, bf16[320,128]{1,0:T(8,128)(2,1)S(1)}, u32[]{:S(2)}, u32[]{:S(2)}) collective-permute-start(bf16[320,128]{1,0:T(8,128)(2,1)S(1)} %get-tuple-element.60), channel_id=1, source_target_pairs={{0,8},{2,10},{4,12},{6,14},{8,0},{10,2},{12,4},{14,6},{16,24},{18,... | collective-permute-start | bytes 245768 | tf_op jit(solution)/shard_map/ppermute | solution.py:259
  152.9 6.6 %collective-permute-done.19 = bf16[320,128]{1,0:T(8,128)(2,1)S(1)} collective-permute-done((bf16[320,128]{1,0:T(8,128)(2,1)S(1)}, bf16[320,128]{1,0:T(8,128)(2,1)S(1)}, u32[]{:S(2)}, u32[]{:S(2)}) %collective-permute-start.19) | collective-permute-done | bytes 81952 | tf_op jit(solution)/shard_map/ppermute | solution.py:259
  162.3 5.5 %collective-permute-done.21 = bf16[320,512]{1,0:T(8,128)(2,1)S(1)} collective-permute-done((bf16[320,512]{1,0:T(8,128)(2,1)S(1)}, bf16[320,512]{1,0:T(8,128)(2,1)S(1)}, u32[]{:S(2)}, u32[]{:S(2)}) %collective-permute-start.21) | collective-permute-done | bytes 327712 | tf_op jit(solution)/shard_map/ppermute | solution.py:265
  168.5 2.3 %fusion.2 = bf16[320,1536]{1,0:T(8,128)(2,1)} fusion(f32[320,1536]{1,0:T(8,128)S(1)} %fusion.50, f32[320,1536]{1,0:T(8,128)S(1)} %fusion.49, f32[320,1536]{1,0:T(8,128)S(1)} %fusion.48, bf16[320,1024]{1,0:T(8,128)(2,1)S(1)} %constant_dynamic-update-slice_fusion, bf16[256,1536]{1,0:T(8,128)(2,1)S(1)} %copy-done.14, bf16[256,1536]{1,0:T(8,128)(2,1)S(1)} %copy-done.15, ...), kind=kOutput, calls=%fused_computation.6 | convolution fusion | flops 1021181952 | bytes 10682368 | tf_op jit(solution)/shard_map/dot_general | solution.py:366
  (112 shorter events, 28.5 us)
Async XLA Ops:
  4.3 18.0 %collective-permute-start.2 = (bf16[3,336,256]{2,1,0:T(8,128)(2,1)}, bf16[3,336,256]{2,1,0:T(8,128)(2,1)S(1)}, u32[]{:S(2)}, u32[]{:S(2)}) collective-permute-start(bf16[3,336,256]{2,1,0:T(8,128)(2,1)} %get-tuple-element.118), channel_id=1, source_target_pairs={{0,24},{2,26},{4,28},{6,30},{8,16},{10,18},{12,20},{14,22},{16,8},... | collective-permute-start | bytes 1548296 | tf_op jit(solution)/shard_map/ppermute | solution.py:259
  9.4 44.3 %collective-permute-start.1 = (bf16[3,336,256]{2,1,0:T(8,128)(2,1)S(1)}, bf16[3,336,256]{2,1,0:T(8,128)(2,1)S(1)}, u32[]{:S(2)}, u32[]{:S(2)}) collective-permute-start(bf16[3,336,256]{2,1,0:T(8,128)(2,1)S(1)} %get-tuple-element.117), channel_id=1, source_target_pairs={{0,16},{2,18},{4,20},{6,22},{8,24},{10,26},{12,28},{14,30},{16,0},... | collective-permute-start | bytes 1548296 | tf_op jit(solution)/shard_map/ppermute | solution.py:259
  9.4 44.3 %collective-permute-start = (bf16[3,336,256]{2,1,0:T(8,128)(2,1)S(1)}, bf16[3,336,256]{2,1,0:T(8,128)(2,1)S(1)}, u32[]{:S(2)}, u32[]{:S(2)}) collective-permute-start(bf16[3,336,256]{2,1,0:T(8,128)(2,1)S(1)} %get-tuple-element.116), channel_id=1, source_target_pairs={{0,8},{2,10},{4,12},{6,14},{8,0},{10,2},{12,4},{14,6},{16,24},{18,... | collective-permute-start | bytes 1548296 | tf_op jit(solution)/shard_map/ppermute | solution.py:259
  13.2 60.7 %collective-permute-start.10 = (bf16[768,1536]{1,0:T(8,128)(2,1)}, bf16[768,1536]{1,0:T(8,128)(2,1)}, u32[]{:S(2)}, u32[]{:S(2)}) collective-permute-start(bf16[768,1536]{1,0:T(8,128)(2,1)} %dynamic_slice.140), channel_id=1, source_target_pairs={{0,1},{1,0},{2,3},{3,2},{4,5},{5,4},{6,7},{7,6},{8,9},{9,8},{10,11... | collective-permute-start | bytes 7077896 | tf_op jit(solution)/shard_map/ppermute | solution.py:265
  19.2 56.2 %copy-start = (bf16[3,336,128]{2,1,0:T(8,128)(2,1)}, bf16[3,336,128]{2,1,0:T(8,128)(2,1)S(1)}, u32[]{:S(2)}) copy-start(bf16[3,336,128]{2,1,0:T(8,128)(2,1)S(1)} %get-tuple-element.49.refs_0_) | copy-start | bytes 774148
  53.9 30.0 %collective-permute-start.3 = (bf16[4,2,320,256]{3,2,1,0:T(8,128)(2,1)S(1)}, bf16[4,2,320,256]{3,2,1,0:T(8,128)(2,1)}, u32[]{:S(2)}, u32[]{:S(2)}) collective-permute-start(bf16[4,2,320,256]{3,2,1,0:T(8,128)(2,1)S(1)} %pad_maximum_fusion.4.refs_4_), channel_id=1, source_target_pairs={{0,4},{2,6},{4,0},{6,2},{8,12},{10,14},{12,8},{14,10},{16,20},{18,... | collective-permute-start | bytes 3932168 | tf_op jit(solution)/shard_map/ppermute | solution.py:259
  55.5 3.0 %collective-permute-start.5 = (bf16[4,2,320,256]{3,2,1,0:T(8,128)(2,1)S(1)}, bf16[4,2,320,256]{3,2,1,0:T(8,128)(2,1)S(1)}, u32[]{:S(2)}, u32[]{:S(2)}) collective-permute-start(bf16[4,2,320,256]{3,2,1,0:T(8,128)(2,1)S(1)} %pad_maximum_fusion.4.refs_4_), channel_id=1, source_target_pairs={{0,2},{2,0},{4,6},{6,4},{8,10},{10,8},{12,14},{14,12},{16,18},{18,... | collective-permute-start | bytes 3932168 | tf_op jit(solution)/shard_map/ppermute | solution.py:259
  55.5 28.4 %collective-permute-start.14 = (bf16[3,336,128]{2,1,0:T(8,128)(2,1)}, bf16[3,336,128]{2,1,0:T(8,128)(2,1)}, u32[]{:S(2)}, u32[]{:S(2)}) collective-permute-start(bf16[3,336,128]{2,1,0:T(8,128)(2,1)} %get-tuple-element.48), channel_id=1, source_target_pairs={{0,24},{2,26},{4,28},{6,30},{8,16},{10,18},{12,20},{14,22},{16,8},... | collective-permute-start | bytes 774152 | tf_op jit(solution)/shard_map/ppermute | solution.py:259
  58.4 26.4 %collective-permute-start.13 = (bf16[3,336,128]{2,1,0:T(8,128)(2,1)}, bf16[3,336,128]{2,1,0:T(8,128)(2,1)}, u32[]{:S(2)}, u32[]{:S(2)}) collective-permute-start(bf16[3,336,128]{2,1,0:T(8,128)(2,1)} %get-tuple-element.47), channel_id=1, source_target_pairs={{0,16},{2,18},{4,20},{6,22},{8,24},{10,26},{12,28},{14,30},{16,0},... | collective-permute-start | bytes 774152 | tf_op jit(solution)/shard_map/ppermute | solution.py:259
  73.8 20.7 %copy-start.4 = (f32[4,2,1,320]{3,2,1,0:T(1,128)}, f32[4,2,1,320]{3,2,1,0:T(1,128)S(1)}, u32[]{:S(2)}) copy-start(f32[4,2,1,320]{3,2,1,0:T(1,128)S(1)} %get-tuple-element.34.refs_6_) | copy-start | bytes 30724
  73.9 58.7 %collective-permute-start.11 = (bf16[768,1536]{1,0:T(8,128)(2,1)}, bf16[768,1536]{1,0:T(8,128)(2,1)}, u32[]{:S(2)}, u32[]{:S(2)}) collective-permute-start(bf16[768,1536]{1,0:T(8,128)(2,1)} %collective-permute-done.10), channel_id=1, source_target_pairs={{0,2},{2,0},{4,6},{6,4},{8,10},{10,8},{12,14},{14,12},{16,18},{18,... | collective-permute-start | bytes 7077896 | tf_op jit(solution)/shard_map/ppermute | solution.py:259
  76.1 9.7 %collective-permute-start.12 = (bf16[3,336,128]{2,1,0:T(8,128)(2,1)}, bf16[3,336,128]{2,1,0:T(8,128)(2,1)S(1)}, u32[]{:S(2)}, u32[]{:S(2)}) collective-permute-start(bf16[3,336,128]{2,1,0:T(8,128)(2,1)} %get-tuple-element.46), channel_id=1, source_target_pairs={{0,8},{2,10},{4,12},{6,14},{8,0},{10,2},{12,4},{14,6},{16,24},{18,... | collective-permute-start | bytes 774152 | tf_op jit(solution)/shard_map/ppermute | solution.py:259
  83.9 13.2 %collective-permute-start.4 = (bf16[4,2,320,256]{3,2,1,0:T(8,128)(2,1)}, bf16[4,2,320,256]{3,2,1,0:T(8,128)(2,1)}, u32[]{:S(2)}, u32[]{:S(2)}) collective-permute-start(bf16[4,2,320,256]{3,2,1,0:T(8,128)(2,1)} %collective-permute-done.3.refs_4_), channel_id=1, source_target_pairs={{0,2},{2,0},{4,6},{6,4},{8,10},{10,8},{12,14},{14,12},{16,18},{18,... | collective-permute-start | bytes 3932168 | tf_op jit(solution)/shard_map/ppermute | solution.py:259
  87.5 25.7 %collective-permute-start.15 = (bf16[4,2,320,128]{3,2,1,0:T(8,128)(2,1)S(1)}, bf16[4,2,320,128]{3,2,1,0:T(8,128)(2,1)S(1)}, u32[]{:S(2)}, u32[]{:S(2)}) collective-permute-start(bf16[4,2,320,128]{3,2,1,0:T(8,128)(2,1)S(1)} %pad_maximum_fusion.5.refs_4_), channel_id=1, source_target_pairs={{0,4},{2,6},{4,0},{6,2},{8,12},{10,14},{12,8},{14,10},{16,20},{18,... | collective-permute-start | bytes 1966088 | tf_op jit(solution)/shard_map/ppermute | solution.py:259
  94.5 24.1 %collective-permute-start.17 = (bf16[4,2,320,128]{3,2,1,0:T(8,128)(2,1)S(1)}, bf16[4,2,320,128]{3,2,1,0:T(8,128)(2,1)}, u32[]{:S(2)}, u32[]{:S(2)}) collective-permute-start(bf16[4,2,320,128]{3,2,1,0:T(8,128)(2,1)S(1)} %pad_maximum_fusion.5.refs_4_), channel_id=1, source_target_pairs={{0,2},{2,0},{4,6},{6,4},{8,10},{10,8},{12,14},{14,12},{16,18},{18,... | collective-permute-start | bytes 1966088 | tf_op jit(solution)/shard_map/ppermute | solution.py:259
  111.8 18.0 %collective-permute-start.6 = (bf16[320,256]{1,0:T(8,128)(2,1)}, bf16[320,256]{1,0:T(8,128)(2,1)S(1)}, u32[]{:S(2)}, u32[]{:S(2)}) collective-permute-start(bf16[320,256]{1,0:T(8,128)(2,1)} %get-tuple-element.38), channel_id=1, source_target_pairs={{0,8},{2,10},{4,12},{6,14},{8,0},{10,2},{12,4},{14,6},{16,24},{18,... | collective-permute-start | bytes 491528 | tf_op jit(solution)/shard_map/ppermute | solution.py:259
  113.2 25.0 %collective-permute-start.16 = (bf16[4,2,320,128]{3,2,1,0:T(8,128)(2,1)S(1)}, bf16[4,2,320,128]{3,2,1,0:T(8,128)(2,1)S(1)}, u32[]{:S(2)}, u32[]{:S(2)}) collective-permute-start(bf16[4,2,320,128]{3,2,1,0:T(8,128)(2,1)S(1)} %collective-permute-done.15.refs_4_), channel_id=1, source_target_pairs={{0,2},{2,0},{4,6},{6,4},{8,10},{10,8},{12,14},{14,12},{16,18},{18,... | collective-permute-start | bytes 1966088 | tf_op jit(solution)/shard_map/ppermute | solution.py:259
  116.1 15.0 %collective-permute-start.7 = (bf16[320,256]{1,0:T(8,128)(2,1)S(1)}, bf16[320,256]{1,0:T(8,128)(2,1)S(1)}, u32[]{:S(2)}, u32[]{:S(2)}) collective-permute-start(bf16[320,256]{1,0:T(8,128)(2,1)S(1)} %copy-done.11), channel_id=1, source_target_pairs={{0,16},{2,18},{4,20},{6,22},{8,24},{10,26},{12,28},{14,30},{16,0},... | collective-permute-start | bytes 491528 | tf_op jit(solution)/shard_map/ppermute | solution.py:259
  118.7 12.4 %collective-permute-start.8 = (bf16[320,256]{1,0:T(8,128)(2,1)S(1)}, bf16[320,256]{1,0:T(8,128)(2,1)S(1)}, u32[]{:S(2)}, u32[]{:S(2)}) collective-permute-start(bf16[320,256]{1,0:T(8,128)(2,1)S(1)} %copy-done.9), channel_id=1, source_target_pairs={{0,24},{2,26},{4,28},{6,30},{8,16},{10,18},{12,20},{14,22},{16,8},... | collective-permute-start | bytes 491528 | tf_op jit(solution)/shard_map/ppermute | solution.py:259
  131.1 29.2 %collective-permute-start.9 = (bf16[320,1024]{1,0:T(8,128)(2,1)S(1)}, bf16[320,1024]{1,0:T(8,128)(2,1)S(1)}, u32[]{:S(2)}, u32[]{:S(2)}) collective-permute-start(bf16[320,1024]{1,0:T(8,128)(2,1)S(1)} %constant_dynamic-update-slice_fusion), channel_id=1, source_target_pairs={{0,1},{1,0},{2,3},{3,2},{4,5},{5,4},{6,7},{7,6},{8,9},{9,8},{10,11... | collective-permute-start | bytes 1966088 | tf_op jit(solution)/shard_map/ppermute | solution.py:265
  146.7 6.2 %collective-permute-start.18 = (bf16[320,128]{1,0:T(8,128)(2,1)S(1)}, bf16[320,128]{1,0:T(8,128)(2,1)S(1)}, u32[]{:S(2)}, u32[]{:S(2)}) collective-permute-start(bf16[320,128]{1,0:T(8,128)(2,1)S(1)} %get-tuple-element.60), channel_id=1, source_target_pairs={{0,8},{2,10},{4,12},{6,14},{8,0},{10,2},{12,4},{14,6},{16,24},{18,... | collective-permute-start | bytes 245768 | tf_op jit(solution)/shard_map/ppermute | solution.py:259
  149.9 9.6 %collective-permute-start.19 = (bf16[320,128]{1,0:T(8,128)(2,1)S(1)}, bf16[320,128]{1,0:T(8,128)(2,1)S(1)}, u32[]{:S(2)}, u32[]{:S(2)}) collective-permute-start(bf16[320,128]{1,0:T(8,128)(2,1)S(1)} %get-tuple-element.61), channel_id=1, source_target_pairs={{0,16},{2,18},{4,20},{6,22},{8,24},{10,26},{12,28},{14,30},{16,0},... | collective-permute-start | bytes 245768 | tf_op jit(solution)/shard_map/ppermute | solution.py:259
  150.8 8.7 %collective-permute-start.20 = (bf16[320,128]{1,0:T(8,128)(2,1)S(1)}, bf16[320,128]{1,0:T(8,128)(2,1)S(1)}, u32[]{:S(2)}, u32[]{:S(2)}) collective-permute-start(bf16[320,128]{1,0:T(8,128)(2,1)S(1)} %get-tuple-element.62), channel_id=1, source_target_pairs={{0,24},{2,26},{4,28},{6,30},{8,16},{10,18},{12,20},{14,22},{16,8},... | collective-permute-start | bytes 245768 | tf_op jit(solution)/shard_map/ppermute | solution.py:259
  159.6 8.1 %collective-permute-start.21 = (bf16[320,512]{1,0:T(8,128)(2,1)S(1)}, bf16[320,512]{1,0:T(8,128)(2,1)S(1)}, u32[]{:S(2)}, u32[]{:S(2)}) collective-permute-start(bf16[320,512]{1,0:T(8,128)(2,1)S(1)} %constant_dynamic-update-slice_fusion.4), channel_id=1, source_target_pairs={{0,1},{1,0},{2,3},{3,2},{4,5},{5,4},{6,7},{7,6},{8,9},{9,8},{10,11... | collective-permute-start | bytes 983048 | tf_op jit(solution)/shard_map/ppermute | solution.py:265
  (16 other events, 93.4 us)
where the time goes:
time: 171 us
  waiting for transfers between devices  54.6 us (32%)
  Pallas kernels  46.6 us (27%)
  starting transfers between devices  31.3 us (18%)
  local copies, waits for them, and re-layouts  22.1 us (13%)
  other arithmetic  10.8 us (6%)
  matrix products  4.81 us (3%)
    ppermute x19, waiting for transfers between devices, swap(): return lax.ppermute(value, 'seq', [(i, i ^ bits) for i in range(blocks)])  49.2 us
    pallas_call x4, Pallas kernels, attend(): pl.pallas_call(functools.partial(attend_kernel, heads, plan, not state, l...  46.6 us
    ppermute x19, starting transfers between devices, swap(): return lax.ppermute(value, 'seq', [(i, i ^ bits) for i in range(blocks)])  27.5 us
    dynamic_slice x4, local copies, waits for them, and re-layouts, weight_rows(): lax.dynamic_slice_in_dim(weight, ((plane ^ k) * per_plane + start) * HD,...  8 us
    another operation x5, local copies, waits for them, and re-layouts, pack_heads(): jnp.stack([lax.dynamic_slice_in_dim(array, first, heads * HD, 1) for arra...  5.85 us
    ppermute x3, waiting for transfers between devices, across(): return lax.ppermute(value, 'head', [(0, 1), (1, 0)])  5.47 us
    select_n x1, other arithmetic, grouped_body(): jnp.where(core == 0, jnp.concatenate([part, rest]), jnp.concatenate([rest...  4.96 us
    ppermute x3, starting transfers between devices, across(): return lax.ppermute(value, 'head', [(0, 1), (1, 0)])  3.87 us
  transfers between devices with their start and end apart: 22, of which 8 were waited for; matrix products, arithmetic and copies ran while one was open for 17% of the time, Pallas kernels for 27%

commit v1 on v0

--- a/solution.py
+++ b/solution.py
@@ -238,7 +238,7 @@
             pltpu.SemaphoreType.DMA((slots,)),
             pltpu.SemaphoreType.DMA((3,)),
         ],
-        compiler_params=pltpu.CompilerParams(vmem_limit_bytes=48 << 20),
+        compiler_params=pltpu.CompilerParams(vmem_limit_bytes=20 << 20),
         cost_estimate=pl.CostEstimate(flops=0, bytes_accessed=0, transcendentals=0),
         name="attend_slots",
     )(flags, *own, *held, *state)
@@ -266,6 +266,9 @@
 
     def after(value, *others):
         return lax.optimization_barrier((value, others))[0]
+
+    def stack(pieces):
+        return jnp.stack([piece[:2, :rows] for piece in pieces])
 
     def pack_heads(arrays, start, heads):
         note = jnp.pad(
@@ -285,36 +288,46 @@
     half = width // 2
     core = index % 2
     packed = [pack_heads(arrays, starts[0], chunks[0])]
+
+    def weight_rows(weight, side_at, away, c):
+        return [
+            lax.dynamic_slice(
+                weight,
+                (((plane ^ k) * per_plane + starts[c]) * HD, side_at * out_cols),
+                (chunks[c] * HD, out_cols),
+            )
+            for k in away
+        ]
+
     weight = after(out_weight, packed[0])
-    theirs = lax.dynamic_slice(weight, (core * half, (1 - side) * out_cols), (half, out_cols))
+    theirs = jnp.concatenate(
+        sum([weight_rows(weight, 1 - side, (2 * core, 2 * core + 1), c) for c in range(len(chunks))], [])
+    )
     part = across(theirs)
+    weight_near = [
+        jnp.concatenate(weight_rows(after(weight, theirs), side, range(PLANES), c))
+        for c in range(len(chunks))
+    ]
     for c in range(1, len(chunks)):
         arrays = after(arrays, packed[-1], theirs)
         packed.append(pack_heads(arrays, starts[c], chunks[c]))
 
-    pieces_all, shared = [], []
-    for c in range(len(chunks)):
-        pieces = packed[c]
-        if c > 0:
-            before = pieces_all[-1]
-            pieces = [
-                pieces[0],
-                after(pieces[1], before[3]),
-                after(pieces[2], before[2]),
-                after(pieces[3], before[1]),
-            ]
+    def receive(pieces, *gate):
         pieces = [pieces[0]] + [swap_planes(pieces[k], k) for k in range(1, PLANES)]
-        mine = jnp.stack([piece[:2, :rows] for piece in pieces])
-        beside = swap(mine, 1)
-        chip = swap(mine, 2)
-        chip_beside = swap(chip, 1)
-        pieces_all.append(pieces)
-        shared.append((mine, beside, chip, chip_beside))
+        low = stack(pieces[:2])
+        chip_low = swap(low, 2)
+        pieces[2:] = after(pieces[2:], *gate) if gate else after(pieces[2:], chip_low, weight_near)
+        high = stack(pieces[2:])
+        chip_high = swap(high, 2)
+        mine = [low, high, swap(low, 1), swap(high, 1)]
+        return pieces, mine, [chip_low, chip_high, swap(chip_low, 1), swap(chip_high, 1)]
+
+    received = [receive(packed[0])]
 
     planes_at = (plane ^ jnp.arange(PLANES, dtype=jnp.int32)) * GROUP
     my_blocks = planes_at + member
     held = jnp.concatenate([planes_at + (member ^ m) for m in range(GROUP)])
-    my_pattern = jnp.stack([piece[0, rows, : 2 * REACH] for piece in pieces_all[0]])
+    my_pattern = jnp.stack([piece[0, rows, : 2 * REACH] for piece in received[0][0]])
     away = (held[None, :] - my_blocks[:, None]) % blocks
     full = (away == 0).astype(jnp.int32)
     for offset in list(range(-REACH, 0)) + list(range(1, REACH + 1)):
@@ -324,47 +337,44 @@
     flags = full + 2 * is_ref[None, :]
     near_flags, far_flags = flags[:, : 2 * PLANES], flags[:, 2 * PLANES :]
 
-    def weight_rows(weight, start, heads):
-        return jnp.concatenate(
-            [
-                lax.dynamic_slice_in_dim(
-                    weight, ((plane ^ k) * per_plane + start) * HD, heads * HD, 0
-                )
-                for k in range(PLANES)
-            ]
-        )
+    def project(mixed, near, far, c, part, rest):
+        mixed = mixed + jnp.dot(near, weight_near[c], preferred_element_type=F32)
+        pair_width = 2 * chunks[c] * HD
+        row = 2 * starts[c] * HD
+        for at, held in ((core, part), (1 - core, rest)):
+            columns = lax.dynamic_slice_in_dim(far, at * pair_width, pair_width, 1)
+            mixed = mixed + jnp.dot(
+                columns, held[row : row + pair_width], preferred_element_type=F32
+            )
+        return mixed
+
+    def hand_back(outs):
+        back = [outs[0]] + [swap_planes(outs[k], k) for k in range(1, PLANES)]
+        return jnp.concatenate(back, axis=1)
 
     mixed = jnp.zeros((rows, out_cols), F32)
-    weights = []
-    done = []
+    rest = outs = None
     for c in range(len(chunks)):
-        own = pieces_all[c]
-        mine, beside, chip, chip_beside = shared[c]
+        own, mine, theirs_now = received[c]
         if c > 0:
-            own = after(own, done[-1])
-        state = attend(near_flags, own, [mine, beside], None, False)
-        if c == 0:
-            part = after(part, state)
+            own = after(own, outs)
+            near_before = hand_back(outs)
+        state = attend(near_flags, own, mine, None, False)
+        if c > 0:
+            near_before, state = lax.optimization_barrier((near_before, state))
+            mixed = project(mixed, near_before, across(near_before), c - 1, part, rest)
+        if c + 1 < len(chunks):
+            coming = [packed[c + 1][0]] + list(
+                after(tuple(packed[c + 1][1:]), own[1], own[2])
+            )
+            received.append(receive(coming, state, part))
+        if rest is None:
             rest = swap(part, 1)
-            weight_far = jnp.where(
-                core == 0, jnp.concatenate([part, rest]), jnp.concatenate([rest, part])
-            )
-            weight_near = lax.dynamic_slice_in_dim(out_weight, side * out_cols, out_cols, 1)
-            weights = [
-                [weight_rows(weight, starts[n], chunks[n]) for weight in (weight_near, weight_far)]
-                for n in range(len(chunks))
-            ]
-        else:
-            state = after(state, weights)
-        outs = attend(far_flags, own, [chip, chip_beside], list(state), True)
-        done.append(outs)
-        near = jnp.concatenate(
-            [outs[0]] + [swap_planes(outs[k], k) for k in range(1, PLANES)], axis=1
-        )
-        far = across(near)
-        weight_n, weight_f = weights[c]
-        mixed = mixed + jnp.dot(near, weight_n, preferred_element_type=F32)
-        mixed = mixed + jnp.dot(far, weight_f, preferred_element_type=F32)
+            state = after(state, rest)
+        outs = attend(far_flags, own, theirs_now, list(state), True)
+    near = hand_back(outs)
+    far, mixed = lax.optimization_barrier((across(near), mixed))
+    mixed = project(mixed, near, far, len(chunks) - 1, part, rest)
     return mixed.astype(BF16)
 
 

time: 171 us -> 167 us (0.977)
  local copies, waits for them, and re-layouts: 22.1 us -> 16.1 us
  matrix products: 4.81 us -> 7.73 us
  other arithmetic: 10.8 us -> 8.92 us
    ppermute x3, waiting for transfers between devices: 5.47 us -> 12.3 us  [across(): return lax.ppermute(value, 'head', [(0, 1), (1, 0)])]
    ppermute x19 -> x25, waiting for transfers between devices: 49.2 us -> 43 us  [swap(): return lax.ppermute(value, 'seq', [(i, i ^ bits) for i in range(blocks)])]
    dynamic_slice x5 -> x4, local copies, waits for them, and re-layouts: 11.3 us -> 6.16 us  [weight_rows(): lax.dynamic_slice(weight, (((plane ^ k) * per_plane + starts[c]) * HD, si...]
    select_n x1 -> x0, other arithmetic: 4.96 us -> none  [grouped_body(): jnp.where(core == 0, jnp.concatenate([part, rest]), jnp.concatenate([rest...]
    concatenate x3 -> x4, other arithmetic: 1.67 us -> 4.78 us  [the longest x2 3.13 us: grouped_body(): jnp.concatenate(weight_rows(after(weight, theirs), side, range(PLANES), c))]
    dot_general x4 -> x6, matrix products: 4.81 us -> 7.73 us  [the longest x4 5.89 us: project(): jnp.dot(columns, held[row:row + pair_width], preferred_element_type=F32)]
    another operation x12, local copies, waits for them, and re-layouts: 2.65 us -> 0.83 us  [the longest x8 0.82 us: stack(): return jnp.stack([piece[:2, :rows] for piece in pieces])]
    pallas_call x4, Pallas kernels: 46.6 us -> 48.3 us  [attend(): pl.pallas_call(functools.partial(attend_kernel, heads, plan, not state, l...]
  transfers between devices with their start and end apart: 22 -> 28, of which waited for: 8 -> 7; matrix products, arithmetic and copies ran while one was open for 17% -> 13% of each run, Pallas kernels for 27% -> 29%
where the time goes in v1:
time: 167 us
  waiting for transfers between devices  55.3 us (33%)
  Pallas kernels  48.3 us (29%)
  starting transfers between devices  30.3 us (18%)
  local copies, waits for them, and re-layouts  16.1 us (10%)
  other arithmetic  8.92 us (5%)
  matrix products  7.73 us (5%)
    pallas_call x4, Pallas kernels, attend(): pl.pallas_call(functools.partial(attend_kernel, heads, plan, not state, l...  48.3 us
    ppermute x25, waiting for transfers between devices, swap(): return lax.ppermute(value, 'seq', [(i, i ^ bits) for i in range(blocks)])  43 us
    ppermute x25, starting transfers between devices, swap(): return lax.ppermute(value, 'seq', [(i, i ^ bits) for i in range(blocks)])  26.6 us
    ppermute x3, waiting for transfers between devices, across(): return lax.ppermute(value, 'head', [(0, 1), (1, 0)])  12.3 us
    dynamic_slice x4, local copies, waits for them, and re-layouts, weight_rows(): lax.dynamic_slice(weight, (((plane ^ k) * per_plane + starts[c]) * HD, si...  6.16 us
    dot_general x4, matrix products, project(): jnp.dot(columns, held[row:row + pair_width], preferred_element_type=F32)  5.89 us
    another operation x5, local copies, waits for them, and re-layouts, pack_heads(): jnp.stack([lax.dynamic_slice_in_dim(array, first, heads * HD, 1) for arra...  5.85 us
    ppermute x3, starting transfers between devices, across(): return lax.ppermute(value, 'head', [(0, 1), (1, 0)])  3.66 us
  transfers between devices with their start and end apart: 28, of which 7 were waited for; matrix products, arithmetic and copies ran while one was open for 13% of the time, Pallas kernels for 29%

profile of v1, /device:TPU:0, one launch (start us, length us, event | category | flops | bytes accessed | tf_op | source)
XLA Modules:
  0.0 167.1 jit_solution(14064813171102164391)
XLA Ops:
  4.5 4.0 %collective-permute-start.1 = (bf16[3,336,256]{2,1,0:T(8,128)(2,1)}, bf16[3,336,256]{2,1,0:T(8,128)(2,1)S(1)}, u32[]{:S(2)}, u32[]{:S(2)}) collective-permute-start(bf16[3,336,256]{2,1,0:T(8,128)(2,1)} %get-tuple-element.133), channel_id=1, source_target_pairs={{0,16},{2,18},{4,20},{6,22},{8,24},{10,26},{12,28},{14,30},{16,0},... | collective-permute-start | bytes 1548296 | tf_op jit(solution)/shard_map/ppermute | solution.py:259
  12.7 1.6 pad_maximum_fusion.1
  22.2 2.1 %fusion.57 = (bf16[256,1536]{1,0:T(8,128)(2,1)S(1)}, bf16[256,1536]{1,0:T(8,128)(2,1)S(1)}, bf16[256,1536]{1,0:T(8,128)(2,1)S(1)}, bf16[256,1536]{1,0:T(8,128)(2,1)S(1)}) fusion(bf16[1536,3072]{1,0:T(8,128)(2,1)} %param.11, s32[]{:T(128)S(6)} %select_n.112, s32[]{:T(128)S(6)} %select_n.122, s32[]{:T(128)S(6)} %select_n.115, s32[]{:T(128)S(6)} %select_n.114, ...), kind=kLoop, calls=%fused_computation.140 | loop fusion | bytes 6291476 | tf_op jit(solution)/shard_map/dynamic_slice | solution.py:294
  24.4 1.8 %pad_maximum_fusion = bf16[1024,1536]{1,0:T(8,128)(2,1)} fusion(bf16[256,1536]{1,0:T(8,128)(2,1)S(1)} %get-tuple-element.94, bf16[256,1536]{1,0:T(8,128)(2,1)S(1)} %get-tuple-element.95, bf16[256,1536]{1,0:T(8,128)(2,1)S(1)} %get-tuple-element.96, bf16[256,1536]{1,0:T(8,128)(2,1)S(1)} %get-tuple-element.93), kind=kLoop, calls=%fused_computation | loop fusion | flops 12582912 | bytes 6291456 | tf_op jit(solution)/shard_map/concatenate | solution.py:308
  26.2 17.7 %collective-permute-done.refs_1_ = bf16[3,336,256]{2,1,0:T(8,128)(2,1)S(1)} collective-permute-done((bf16[3,336,256]{2,1,0:T(8,128)(2,1)}, bf16[3,336,256]{2,1,0:T(8,128)(2,1)S(1)}, u32[]{:S(2)}, u32[]{:S(2)}) %collective-permute-start) | collective-permute-done | bytes 516128 | tf_op jit(solution)/shard_map/ppermute | solution.py:259
  44.0 1.6 collective-permute-start.3
  47.0 10.8 %collective-permute-done.3.refs_4_ = bf16[2,2,320,256]{3,2,1,0:T(8,128)(2,1)S(1)} collective-permute-done((bf16[2,2,320,256]{3,2,1,0:T(8,128)(2,1)S(1)}, bf16[2,2,320,256]{3,2,1,0:T(8,128)(2,1)S(1)}, u32[]{:S(2)}, u32[]{:S(2)}) %collective-permute-start.3) | collective-permute-done | bytes 655392 | tf_op jit(solution)/shard_map/ppermute | solution.py:259
  57.8 9.2 %collective-permute-done.9 = bf16[768,1536]{1,0:T(8,128)(2,1)} collective-permute-done((bf16[768,1536]{1,0:T(8,128)(2,1)}, bf16[768,1536]{1,0:T(8,128)(2,1)}, u32[]{:S(2)}, u32[]{:S(2)}) %collective-permute-start.9) | collective-permute-done | bytes 2359328 | tf_op jit(solution)/shard_map/ppermute | solution.py:265
  67.7 1.5 collective-permute-start.10
  69.3 1.5 collective-permute-start.4
  71.2 1.7 %collective-permute-start.5 = (bf16[3,336,128]{2,1,0:T(8,128)(2,1)}, bf16[3,336,128]{2,1,0:T(8,128)(2,1)S(1)}, u32[]{:S(2)}, u32[]{:S(2)}) collective-permute-start(bf16[3,336,128]{2,1,0:T(8,128)(2,1)} %get-tuple-element.52), channel_id=1, source_target_pairs={{0,16},{2,18},{4,20},{6,22},{8,24},{10,26},{12,28},{14,30},{16,0},... | collective-permute-start | bytes 774152 | tf_op jit(solution)/shard_map/ppermute | solution.py:259
  72.9 9.0 %collective-permute-done.4.refs_1_ = bf16[3,336,128]{2,1,0:T(8,128)(2,1)S(1)} collective-permute-done((bf16[3,336,128]{2,1,0:T(8,128)(2,1)S(1)}, bf16[3,336,128]{2,1,0:T(8,128)(2,1)S(1)}, u32[]{:S(2)}, u32[]{:S(2)}) %collective-permute-start.4) | collective-permute-done | bytes 258080 | tf_op jit(solution)/shard_map/ppermute | solution.py:259
  83.6 14.1 %attend_slots.4 = (f32[4,2,1,320]{3,2,1,0:T(1,128)S(1)}, f32[4,2,1,320]{3,2,1,0:T(1,128)S(1)}, f32[4,2,128,320]{3,2,1,0:T(8,128)S(1)}) custom-call(s32[4,8]{1,0:T(4,128)S(1)} %get-tuple-element.125.flags_ref, bf16[3,336,256]{2,1,0:T(8,128)(2,1)S(1)} %get-tuple-element.134.refs_0_, bf16[3,336,256]{2,1,0:T(8,128)(2,1)S(1)} %collective-permute-done.refs_1_, ...), custom_call_target="tpu_custom_call" | custom-call | tf_op jit(solution)/shard_map/attend_slots/pallas_call | solution.py:223
  100.6 1.6 collective-permute-start.15
  102.4 15.2 %attend_slots.5 = (bf16[320,256]{1,0:T(8,128)(2,1)S(1)}, bf16[320,256]{1,0:T(8,128)(2,1)}, bf16[320,256]{1,0:T(8,128)(2,1)}, bf16[320,256]{1,0:T(8,128)(2,1)}) custom-call(s32[4,8]{1,0:T(4,128)S(1)} %get-tuple-element.126.flags_ref, bf16[3,336,256]{2,1,0:T(8,128)(2,1)S(1)} %get-tuple-element.134.refs_0_, ...), custom_call_target="tpu_custom_call" | custom-call | tf_op jit(solution)/shard_map/attend_slots/pallas_call | solution.py:223
  118.2 2.3 %collective-permute-start.20 = (bf16[320,256]{1,0:T(8,128)(2,1)}, bf16[320,256]{1,0:T(8,128)(2,1)S(1)}, u32[]{:S(2)}, u32[]{:S(2)}) collective-permute-start(bf16[320,256]{1,0:T(8,128)(2,1)} %get-tuple-element.65), channel_id=1, source_target_pairs={{0,24},{2,26},{4,28},{6,30},{8,16},{10,18},{12,20},{14,22},{16,8},... | collective-permute-start | bytes 491528 | tf_op jit(solution)/shard_map/ppermute | solution.py:259
  124.9 9.6 %attend_slots.6 = (f32[4,1,1,320]{3,2,1,0:T(1,128)S(1)}, f32[4,1,1,320]{3,2,1,0:T(1,128)S(1)}, f32[4,1,128,320]{3,2,1,0:T(8,128)S(1)}) custom-call(s32[4,8]{1,0:T(4,128)S(1)} %get-tuple-element.125.flags_ref, bf16[3,336,128]{2,1,0:T(8,128)(2,1)S(1)} %get-tuple-element.66.refs_0_, bf16[3,336,128]{2,1,0:T(8,128)(2,1)S(1)} %collective-permute-done.4.refs_1_, ...), custom_call_target="tpu_custom_call" | custom-call | tf_op jit(solution)/shard_map/attend_slots/pallas_call | solution.py:223
  134.6 1.6 collective-permute-start.27
  137.4 9.4 %attend_slots.7 = (bf16[320,128]{1,0:T(8,128)(2,1)S(1)}, bf16[320,128]{1,0:T(8,128)(2,1)S(1)}, bf16[320,128]{1,0:T(8,128)(2,1)S(1)}, bf16[320,128]{1,0:T(8,128)(2,1)S(1)}) custom-call(s32[4,8]{1,0:T(4,128)S(1)} %get-tuple-element.126.flags_ref, bf16[3,336,128]{2,1,0:T(8,128)(2,1)S(1)} %get-tuple-element.66.refs_0_, ...), custom_call_target="tpu_custom_call" | custom-call | tf_op jit(solution)/shard_map/attend_slots/pallas_call | solution.py:223
  147.5 2.2 %collective-permute-start.24 = (bf16[320,128]{1,0:T(8,128)(2,1)S(1)}, bf16[320,128]{1,0:T(8,128)(2,1)S(1)}, u32[]{:S(2)}, u32[]{:S(2)}) collective-permute-start(bf16[320,128]{1,0:T(8,128)(2,1)S(1)} %get-tuple-element.78), channel_id=1, source_target_pairs={{0,16},{2,18},{4,20},{6,22},{8,24},{10,26},{12,28},{14,30},{16,0},... | collective-permute-start | bytes 245768 | tf_op jit(solution)/shard_map/ppermute | solution.py:259
  152.2 4.5 %collective-permute-done.24 = bf16[320,128]{1,0:T(8,128)(2,1)S(1)} collective-permute-done((bf16[320,128]{1,0:T(8,128)(2,1)S(1)}, bf16[320,128]{1,0:T(8,128)(2,1)S(1)}, u32[]{:S(2)}, u32[]{:S(2)}) %collective-permute-start.24) | collective-permute-done | bytes 81952 | tf_op jit(solution)/shard_map/ppermute | solution.py:259
  158.1 2.2 %convolution_add_fusion.1 = f32[320,1536]{1,0:T(8,128)S(1)} fusion(f32[320,1536]{1,0:T(8,128)S(1)} %fusion.61, bf16[768,1536]{1,0:T(8,128)(2,1)} %collective-permute-done.9, bf16[320,1024]{1,0:T(8,128)(2,1)S(1)} %collective-permute-done.27, s32[]{:T(128)S(6)} %select_n.127), kind=kOutput, calls=%fused_computation.2 | convolution fusion | flops 503808000 | bytes 5832708 | tf_op jit(solution)/shard_map/dot_general | solution.py:346
  161.0 3.1 %collective-permute-done.26 = bf16[320,512]{1,0:T(8,128)(2,1)S(1)} collective-permute-done((bf16[320,512]{1,0:T(8,128)(2,1)S(1)}, bf16[320,512]{1,0:T(8,128)(2,1)S(1)}, u32[]{:S(2)}, u32[]{:S(2)}) %collective-permute-start.26) | collective-permute-done | bytes 327712 | tf_op jit(solution)/shard_map/ppermute | solution.py:265
  164.1 1.6 fusion.16
  (111 shorter events, 36.6 us)
Async XLA Ops:
  4.5 42.5 %collective-permute-start.1 = (bf16[3,336,256]{2,1,0:T(8,128)(2,1)}, bf16[3,336,256]{2,1,0:T(8,128)(2,1)S(1)}, u32[]{:S(2)}, u32[]{:S(2)}) collective-permute-start(bf16[3,336,256]{2,1,0:T(8,128)(2,1)} %get-tuple-element.133), channel_id=1, source_target_pairs={{0,16},{2,18},{4,20},{6,22},{8,24},{10,26},{12,28},{14,30},{16,0},... | collective-permute-start | bytes 1548296 | tf_op jit(solution)/shard_map/ppermute | solution.py:259
  8.5 38.5 %collective-permute-start.2 = (bf16[3,336,256]{2,1,0:T(8,128)(2,1)S(1)}, bf16[3,336,256]{2,1,0:T(8,128)(2,1)S(1)}, u32[]{:S(2)}, u32[]{:S(2)}) collective-permute-start(bf16[3,336,256]{2,1,0:T(8,128)(2,1)S(1)} %get-tuple-element.131), channel_id=1, source_target_pairs={{0,24},{2,26},{4,28},{6,30},{8,16},{10,18},{12,20},{14,22},{16,8},... | collective-permute-start | bytes 1548296 | tf_op jit(solution)/shard_map/ppermute | solution.py:259
  9.9 34.1 %collective-permute-start = (bf16[3,336,256]{2,1,0:T(8,128)(2,1)}, bf16[3,336,256]{2,1,0:T(8,128)(2,1)S(1)}, u32[]{:S(2)}, u32[]{:S(2)}) collective-permute-start(bf16[3,336,256]{2,1,0:T(8,128)(2,1)} %get-tuple-element.132), channel_id=1, source_target_pairs={{0,8},{2,10},{4,12},{6,14},{8,0},{10,2},{12,4},{14,6},{16,24},{18,... | collective-permute-start | bytes 1548296 | tf_op jit(solution)/shard_map/ppermute | solution.py:259
  14.3 52.7 %collective-permute-start.9 = (bf16[768,1536]{1,0:T(8,128)(2,1)}, bf16[768,1536]{1,0:T(8,128)(2,1)}, u32[]{:S(2)}, u32[]{:S(2)}) collective-permute-start(bf16[768,1536]{1,0:T(8,128)(2,1)} %pad_maximum_fusion.1), channel_id=1, source_target_pairs={{0,1},{1,0},{2,3},{3,2},{4,5},{5,4},{6,7},{7,6},{8,9},{9,8},{10,11... | collective-permute-start | bytes 7077896 | tf_op jit(solution)/shard_map/ppermute | solution.py:265
  44.0 13.8 %collective-permute-start.3 = (bf16[2,2,320,256]{3,2,1,0:T(8,128)(2,1)S(1)}, bf16[2,2,320,256]{3,2,1,0:T(8,128)(2,1)S(1)}, u32[]{:S(2)}, u32[]{:S(2)}) collective-permute-start(bf16[2,2,320,256]{3,2,1,0:T(8,128)(2,1)S(1)} %pad_maximum_fusion.3.refs_4_), channel_id=1, source_target_pairs={{0,4},{2,6},{4,0},{6,2},{8,12},{10,14},{12,8},{14,10},{16,20},{18,... | collective-permute-start | bytes 1966088 | tf_op jit(solution)/shard_map/ppermute | solution.py:259
  47.0 24.2 %collective-permute-start.7 = (bf16[2,2,320,256]{3,2,1,0:T(8,128)(2,1)S(1)}, bf16[2,2,320,256]{3,2,1,0:T(8,128)(2,1)S(1)}, u32[]{:S(2)}, u32[]{:S(2)}) collective-permute-start(bf16[2,2,320,256]{3,2,1,0:T(8,128)(2,1)S(1)} %pad_maximum_fusion.3.refs_4_), channel_id=1, source_target_pairs={{0,2},{2,0},{4,6},{6,4},{8,10},{10,8},{12,14},{14,12},{16,18},{18,... | collective-permute-start | bytes 1966088 | tf_op jit(solution)/shard_map/ppermute | solution.py:259
  67.1 35.1 %collective-permute-start.13 = (bf16[768,1536]{1,0:T(8,128)(2,1)}, bf16[768,1536]{1,0:T(8,128)(2,1)S(1)}, u32[]{:S(2)}, u32[]{:S(2)}) collective-permute-start(bf16[768,1536]{1,0:T(8,128)(2,1)} %collective-permute-done.9), channel_id=1, source_target_pairs={{0,2},{2,0},{4,6},{6,4},{8,10},{10,8},{12,14},{14,12},{16,18},{18,... | collective-permute-start | bytes 7077896 | tf_op jit(solution)/shard_map/ppermute | solution.py:259
  67.2 16.3 %collective-permute-start.8 = (bf16[2,2,320,256]{3,2,1,0:T(8,128)(2,1)S(1)}, bf16[2,2,320,256]{3,2,1,0:T(8,128)(2,1)S(1)}, u32[]{:S(2)}, u32[]{:S(2)}) collective-permute-start(bf16[2,2,320,256]{3,2,1,0:T(8,128)(2,1)S(1)} %pad_maximum_fusion.4.refs_5_), channel_id=1, source_target_pairs={{0,2},{2,0},{4,6},{6,4},{8,10},{10,8},{12,14},{14,12},{16,18},{18,... | collective-permute-start | bytes 1966088 | tf_op jit(solution)/shard_map/ppermute | solution.py:259
  67.7 31.9 %collective-permute-start.10 = (bf16[2,2,320,256]{3,2,1,0:T(8,128)(2,1)S(1)}, bf16[2,2,320,256]{3,2,1,0:T(8,128)(2,1)S(1)}, u32[]{:S(2)}, u32[]{:S(2)}) collective-permute-start(bf16[2,2,320,256]{3,2,1,0:T(8,128)(2,1)S(1)} %pad_maximum_fusion.4.refs_5_), channel_id=1, source_target_pairs={{0,4},{2,6},{4,0},{6,2},{8,12},{10,14},{12,8},{14,10},{16,20},{18,... | collective-permute-start | bytes 1966088 | tf_op jit(solution)/shard_map/ppermute | solution.py:259
  69.3 12.7 %collective-permute-start.4 = (bf16[3,336,128]{2,1,0:T(8,128)(2,1)S(1)}, bf16[3,336,128]{2,1,0:T(8,128)(2,1)S(1)}, u32[]{:S(2)}, u32[]{:S(2)}) collective-permute-start(bf16[3,336,128]{2,1,0:T(8,128)(2,1)S(1)} %get-tuple-element.51), channel_id=1, source_target_pairs={{0,8},{2,10},{4,12},{6,14},{8,0},{10,2},{12,4},{14,6},{16,24},{18,... | collective-permute-start | bytes 774152 | tf_op jit(solution)/shard_map/ppermute | solution.py:259
  71.2 26.5 %collective-permute-start.5 = (bf16[3,336,128]{2,1,0:T(8,128)(2,1)}, bf16[3,336,128]{2,1,0:T(8,128)(2,1)S(1)}, u32[]{:S(2)}, u32[]{:S(2)}) collective-permute-start(bf16[3,336,128]{2,1,0:T(8,128)(2,1)} %get-tuple-element.52), channel_id=1, source_target_pairs={{0,16},{2,18},{4,20},{6,22},{8,24},{10,26},{12,28},{14,30},{16,0},... | collective-permute-start | bytes 774152 | tf_op jit(solution)/shard_map/ppermute | solution.py:259
  81.9 16.4 %collective-permute-start.6 = (bf16[3,336,128]{2,1,0:T(8,128)(2,1)}, bf16[3,336,128]{2,1,0:T(8,128)(2,1)S(1)}, u32[]{:S(2)}, u32[]{:S(2)}) collective-permute-start(bf16[3,336,128]{2,1,0:T(8,128)(2,1)} %get-tuple-element.53), channel_id=1, source_target_pairs={{0,24},{2,26},{4,28},{6,30},{8,16},{10,18},{12,20},{14,22},{16,8},... | collective-permute-start | bytes 774152 | tf_op jit(solution)/shard_map/ppermute | solution.py:259
  83.5 17.1 %collective-permute-start.11 = (bf16[2,2,320,256]{3,2,1,0:T(8,128)(2,1)S(1)}, bf16[2,2,320,256]{3,2,1,0:T(8,128)(2,1)S(1)}, u32[]{:S(2)}, u32[]{:S(2)}) collective-permute-start(bf16[2,2,320,256]{3,2,1,0:T(8,128)(2,1)S(1)} %collective-permute-done.3.refs_4_), channel_id=1, source_target_pairs={{0,2},{2,0},{4,6},{6,4},{8,10},{10,8},{12,14},{14,12},{16,18},{18,... | collective-permute-start | bytes 1966088 | tf_op jit(solution)/shard_map/ppermute | solution.py:259
  97.7 22.8 %collective-permute-start.14 = (bf16[2,2,320,128]{3,2,1,0:T(8,128)(2,1)S(1)}, bf16[2,2,320,128]{3,2,1,0:T(8,128)(2,1)S(1)}, u32[]{:S(2)}, u32[]{:S(2)}) collective-permute-start(bf16[2,2,320,128]{3,2,1,0:T(8,128)(2,1)S(1)} %pad_maximum_fusion.6.refs_4_), channel_id=1, source_target_pairs={{0,4},{2,6},{4,0},{6,2},{8,12},{10,14},{12,8},{14,10},{16,20},{18,... | collective-permute-start | bytes 983048 | tf_op jit(solution)/shard_map/ppermute | solution.py:259
  98.3 22.3 %collective-permute-start.21 = (bf16[2,2,320,128]{3,2,1,0:T(8,128)(2,1)S(1)}, bf16[2,2,320,128]{3,2,1,0:T(8,128)(2,1)S(1)}, u32[]{:S(2)}, u32[]{:S(2)}) collective-permute-start(bf16[2,2,320,128]{3,2,1,0:T(8,128)(2,1)S(1)} %pad_maximum_fusion.6.refs_4_), channel_id=1, source_target_pairs={{0,2},{2,0},{4,6},{6,4},{8,10},{10,8},{12,14},{14,12},{16,18},{18,... | collective-permute-start | bytes 983048 | tf_op jit(solution)/shard_map/ppermute | solution.py:259
  100.6 22.8 %collective-permute-start.15 = (bf16[2,2,320,128]{3,2,1,0:T(8,128)(2,1)}, bf16[2,2,320,128]{3,2,1,0:T(8,128)(2,1)}, u32[]{:S(2)}, u32[]{:S(2)}) collective-permute-start(bf16[2,2,320,128]{3,2,1,0:T(8,128)(2,1)} %pad_maximum_fusion.7.refs_5_), channel_id=1, source_target_pairs={{0,4},{2,6},{4,0},{6,2},{8,12},{10,14},{12,8},{14,10},{16,20},{18,... | collective-permute-start | bytes 983048 | tf_op jit(solution)/shard_map/ppermute | solution.py:259
  102.2 21.2 %collective-permute-start.22 = (bf16[2,2,320,128]{3,2,1,0:T(8,128)(2,1)}, bf16[2,2,320,128]{3,2,1,0:T(8,128)(2,1)}, u32[]{:S(2)}, u32[]{:S(2)}) collective-permute-start(bf16[2,2,320,128]{3,2,1,0:T(8,128)(2,1)} %pad_maximum_fusion.7.refs_5_), channel_id=1, source_target_pairs={{0,2},{2,0},{4,6},{6,4},{8,10},{10,8},{12,14},{14,12},{16,18},{18,... | collective-permute-start | bytes 983048 | tf_op jit(solution)/shard_map/ppermute | solution.py:259
  118.2 16.2 %collective-permute-start.20 = (bf16[320,256]{1,0:T(8,128)(2,1)}, bf16[320,256]{1,0:T(8,128)(2,1)S(1)}, u32[]{:S(2)}, u32[]{:S(2)}) collective-permute-start(bf16[320,256]{1,0:T(8,128)(2,1)} %get-tuple-element.65), channel_id=1, source_target_pairs={{0,24},{2,26},{4,28},{6,30},{8,16},{10,18},{12,20},{14,22},{16,8},... | collective-permute-start | bytes 491528 | tf_op jit(solution)/shard_map/ppermute | solution.py:259
  120.6 13.9 %collective-permute-start.19 = (bf16[320,256]{1,0:T(8,128)(2,1)}, bf16[320,256]{1,0:T(8,128)(2,1)S(1)}, u32[]{:S(2)}, u32[]{:S(2)}) collective-permute-start(bf16[320,256]{1,0:T(8,128)(2,1)} %get-tuple-element.64), channel_id=1, source_target_pairs={{0,16},{2,18},{4,20},{6,22},{8,24},{10,26},{12,28},{14,30},{16,0},... | collective-permute-start | bytes 491528 | tf_op jit(solution)/shard_map/ppermute | solution.py:259
  122.0 12.5 %collective-permute-start.18 = (bf16[320,256]{1,0:T(8,128)(2,1)}, bf16[320,256]{1,0:T(8,128)(2,1)S(1)}, u32[]{:S(2)}, u32[]{:S(2)}) collective-permute-start(bf16[320,256]{1,0:T(8,128)(2,1)} %get-tuple-element.63), channel_id=1, source_target_pairs={{0,8},{2,10},{4,12},{6,14},{8,0},{10,2},{12,4},{14,6},{16,24},{18,... | collective-permute-start | bytes 491528 | tf_op jit(solution)/shard_map/ppermute | solution.py:259
  123.4 14.0 %collective-permute-start.16 = (bf16[2,2,320,128]{3,2,1,0:T(8,128)(2,1)}, bf16[2,2,320,128]{3,2,1,0:T(8,128)(2,1)S(1)}, u32[]{:S(2)}, u32[]{:S(2)}) collective-permute-start(bf16[2,2,320,128]{3,2,1,0:T(8,128)(2,1)} %copy-done), channel_id=1, source_target_pairs={{0,2},{2,0},{4,6},{6,4},{8,10},{10,8},{12,14},{14,12},{16,18},{18,... | collective-permute-start | bytes 983048 | tf_op jit(solution)/shard_map/ppermute | solution.py:259
  123.4 14.0 %collective-permute-start.17 = (bf16[2,2,320,128]{3,2,1,0:T(8,128)(2,1)}, bf16[2,2,320,128]{3,2,1,0:T(8,128)(2,1)S(1)}, u32[]{:S(2)}, u32[]{:S(2)}) collective-permute-start(bf16[2,2,320,128]{3,2,1,0:T(8,128)(2,1)} %collective-permute-done.15.refs_5_), channel_id=1, source_target_pairs={{0,2},{2,0},{4,6},{6,4},{8,10},{10,8},{12,14},{14,12},{16,18},{18,... | collective-permute-start | bytes 983048 | tf_op jit(solution)/shard_map/ppermute | solution.py:259
  134.6 23.5 %collective-permute-start.27 = (bf16[320,1024]{1,0:T(8,128)(2,1)S(1)}, bf16[320,1024]{1,0:T(8,128)(2,1)S(1)}, u32[]{:S(2)}, u32[]{:S(2)}) collective-permute-start(bf16[320,1024]{1,0:T(8,128)(2,1)S(1)} %pad_maximum_fusion.5), channel_id=1, source_target_pairs={{0,1},{1,0},{2,3},{3,2},{4,5},{5,4},{6,7},{7,6},{8,9},{9,8},{10,11... | collective-permute-start | bytes 1966088 | tf_op jit(solution)/shard_map/ppermute | solution.py:265
  147.5 9.2 %collective-permute-start.24 = (bf16[320,128]{1,0:T(8,128)(2,1)S(1)}, bf16[320,128]{1,0:T(8,128)(2,1)S(1)}, u32[]{:S(2)}, u32[]{:S(2)}) collective-permute-start(bf16[320,128]{1,0:T(8,128)(2,1)S(1)} %get-tuple-element.78), channel_id=1, source_target_pairs={{0,16},{2,18},{4,20},{6,22},{8,24},{10,26},{12,28},{14,30},{16,0},... | collective-permute-start | bytes 245768 | tf_op jit(solution)/shard_map/ppermute | solution.py:259
  (16 other events, 126.9 us)

commit v2 on v1

--- a/solution.py
+++ b/solution.py
@@ -300,23 +300,30 @@
         ]
 
     weight = after(out_weight, packed[0])
-    theirs = jnp.concatenate(
-        sum([weight_rows(weight, 1 - side, (2 * core, 2 * core + 1), c) for c in range(len(chunks))], [])
-    )
-    part = across(theirs)
-    weight_near = [
-        jnp.concatenate(weight_rows(after(weight, theirs), side, range(PLANES), c))
-        for c in range(len(chunks))
+    weight_sides = [
+        [
+            jnp.concatenate(weight_rows(weight, at, range(PLANES), c))
+            for c in range(len(chunks))
+        ]
+        for at in (side, 1 - side)
     ]
+    final = len(chunks) - 1
+    part = across(
+        jnp.concatenate(weight_rows(weight, 1 - side, (2 * core, 2 * core + 1), final))
+    )
+    rest = swap(part, 1)
     for c in range(1, len(chunks)):
-        arrays = after(arrays, packed[-1], theirs)
+        arrays = after(arrays, packed[-1])
         packed.append(pack_heads(arrays, starts[c], chunks[c]))
 
     def receive(pieces, *gate):
         pieces = [pieces[0]] + [swap_planes(pieces[k], k) for k in range(1, PLANES)]
+        if gate:
+            pieces[1:] = after(pieces[1:], *gate)
         low = stack(pieces[:2])
         chip_low = swap(low, 2)
-        pieces[2:] = after(pieces[2:], *gate) if gate else after(pieces[2:], chip_low, weight_near)
+        if not gate:
+            pieces[2:] = after(pieces[2:], chip_low, weight_sides, rest)
         high = stack(pieces[2:])
         chip_high = swap(high, 2)
         mine = [low, high, swap(low, 1), swap(high, 1)]
@@ -337,23 +344,15 @@
     flags = full + 2 * is_ref[None, :]
     near_flags, far_flags = flags[:, : 2 * PLANES], flags[:, 2 * PLANES :]
 
-    def project(mixed, near, far, c, part, rest):
-        mixed = mixed + jnp.dot(near, weight_near[c], preferred_element_type=F32)
-        pair_width = 2 * chunks[c] * HD
-        row = 2 * starts[c] * HD
-        for at, held in ((core, part), (1 - core, rest)):
-            columns = lax.dynamic_slice_in_dim(far, at * pair_width, pair_width, 1)
-            mixed = mixed + jnp.dot(
-                columns, held[row : row + pair_width], preferred_element_type=F32
-            )
-        return mixed
+    def project(total, near, at, c):
+        return total + jnp.dot(near, weight_sides[at][c], preferred_element_type=F32)
 
     def hand_back(outs):
         back = [outs[0]] + [swap_planes(outs[k], k) for k in range(1, PLANES)]
         return jnp.concatenate(back, axis=1)
 
-    mixed = jnp.zeros((rows, out_cols), F32)
-    rest = outs = None
+    kept = given = jnp.zeros((rows, out_cols), F32)
+    outs = None
     for c in range(len(chunks)):
         own, mine, theirs_now = received[c]
         if c > 0:
@@ -362,19 +361,26 @@
         state = attend(near_flags, own, mine, None, False)
         if c > 0:
             near_before, state = lax.optimization_barrier((near_before, state))
-            mixed = project(mixed, near_before, across(near_before), c - 1, part, rest)
+            kept = project(kept, near_before, 0, c - 1)
+            given = project(given, near_before, 1, c - 1)
         if c + 1 < len(chunks):
             coming = [packed[c + 1][0]] + list(
                 after(tuple(packed[c + 1][1:]), own[1], own[2])
             )
-            received.append(receive(coming, state, part))
-        if rest is None:
-            rest = swap(part, 1)
-            state = after(state, rest)
+            received.append(receive(coming, state))
+            state = after(state, received[-1][1][0])
         outs = attend(far_flags, own, theirs_now, list(state), True)
     near = hand_back(outs)
-    far, mixed = lax.optimization_barrier((across(near), mixed))
-    mixed = project(mixed, near, far, len(chunks) - 1, part, rest)
+    far = across(near)
+    mixed = project(kept, near, 0, final)
+    if final > 0:
+        taken = across(given.astype(BF16))
+        mixed = mixed + taken.astype(F32)
+    far, mixed = lax.optimization_barrier((far, mixed))
+    pair_width = far.shape[1] // 2
+    for at, held_rows in ((core, part), (1 - core, rest)):
+        columns = lax.dynamic_slice_in_dim(far, at * pair_width, pair_width, 1)
+        mixed = mixed + jnp.dot(columns, held_rows, preferred_element_type=F32)
     return mixed.astype(BF16)
 
 

time: 167 us -> 159 us (0.952)
  Pallas kernels: 48.3 us -> 41.7 us
  other arithmetic: 8.92 us -> 4.8 us
  starting transfers between devices: 30.3 us -> 33.9 us
  local copies, waits for them, and re-layouts: 16.1 us -> 13.2 us
    pallas_call x4, Pallas kernels: 48.3 us -> 41.7 us  [attend(): pl.pallas_call(functools.partial(attend_kernel, heads, plan, not state, l...]
    ppermute x25, waiting for transfers between devices: 43 us -> 48.9 us  [swap(): return lax.ppermute(value, 'seq', [(i, i ^ bits) for i in range(blocks)])]
    ppermute x3, waiting for transfers between devices: 12.3 us -> 7.11 us  [across(): return lax.ppermute(value, 'head', [(0, 1), (1, 0)])]
    ppermute x25, starting transfers between devices: 26.6 us -> 30.2 us  [swap(): return lax.ppermute(value, 'seq', [(i, i ^ bits) for i in range(blocks)])]
    concatenate x3, other arithmetic: 4.7 us -> 2.14 us  [the longest x2 2.09 us: grouped_body(): jnp.concatenate(weight_rows(weight, at, range(PLANES), c))]
    unnamed x27 -> x21, local copies, waits for them, and re-layouts: 3.17 us -> 1.02 us
    dot_general x6 -> x5, matrix products: 7.73 us -> 9.38 us  [the longest x3 6.39 us: project(): jnp.dot(near, weight_sides[at][c], preferred_element_type=F32)]
    dynamic_slice x4 -> x2, local copies, waits for them, and re-layouts: 6.16 us -> 6.07 us  [weight_rows(): lax.dynamic_slice(weight, (((plane ^ k) * per_plane + starts[c]) * HD, si...]
  transfers between devices with their start and end apart: 28 -> 28, of which waited for: 7 -> 8; matrix products, arithmetic and copies ran while one was open for 13% -> 12% of each run, Pallas kernels for 29% -> 26%
where the time goes in v2:
time: 159 us
  waiting for transfers between devices  56 us (35%)
  Pallas kernels  41.7 us (26%)
  starting transfers between devices  33.9 us (21%)
  local copies, waits for them, and re-layouts  13.2 us (8%)
  matrix products  9.38 us (6%)
  other arithmetic  4.8 us (3%)
    ppermute x25, waiting for transfers between devices, swap(): return lax.ppermute(value, 'seq', [(i, i ^ bits) for i in range(blocks)])  48.9 us
    pallas_call x4, Pallas kernels, attend(): pl.pallas_call(functools.partial(attend_kernel, heads, plan, not state, l...  41.7 us
    ppermute x25, starting transfers between devices, swap(): return lax.ppermute(value, 'seq', [(i, i ^ bits) for i in range(blocks)])  30.2 us
    ppermute x3, waiting for transfers between devices, across(): return lax.ppermute(value, 'head', [(0, 1), (1, 0)])  7.11 us
    dot_general x3, matrix products, project(): jnp.dot(near, weight_sides[at][c], preferred_element_type=F32)  6.39 us
    dynamic_slice x2, local copies, waits for them, and re-layouts, weight_rows(): lax.dynamic_slice(weight, (((plane ^ k) * per_plane + starts[c]) * HD, si...  6.07 us
    another operation x5, local copies, waits for them, and re-layouts, pack_heads(): jnp.stack([lax.dynamic_slice_in_dim(array, first, heads * HD, 1) for arra...  5.83 us
    ppermute x3, starting transfers between devices, across(): return lax.ppermute(value, 'head', [(0, 1), (1, 0)])  3.66 us
  transfers between devices with their start and end apart: 28, of which 8 were waited for; matrix products, arithmetic and copies ran while one was open for 12% of the time, Pallas kernels for 26%

profile of v2, /device:TPU:0, one launch (start us, length us, event | category | flops | bytes accessed | tf_op | source)
XLA Modules:
  0.0 159.3 jit_solution(5747615088209143717)
XLA Ops:
  4.5 4.0 %collective-permute-start.1 = (bf16[3,336,256]{2,1,0:T(8,128)(2,1)}, bf16[3,336,256]{2,1,0:T(8,128)(2,1)S(1)}, u32[]{:S(2)}, u32[]{:S(2)}) collective-permute-start(bf16[3,336,256]{2,1,0:T(8,128)(2,1)} %get-tuple-element.135), channel_id=1, source_target_pairs={{0,16},{2,18},{4,20},{6,22},{8,24},{10,26},{12,28},{14,30},{16,0},... | collective-permute-start | bytes 1548296 | tf_op jit(solution)/shard_map/ppermute | solution.py:259
  10.1 2.8 %fusion.49 = (bf16[128,1536]{1,0:T(8,128)(2,1)}, bf16[128,1536]{1,0:T(8,128)(2,1)S(1)}, bf16[128,1536]{1,0:T(8,128)(2,1)S(1)}, bf16[128,1536]{1,0:T(8,128)(2,1)}...) fusion(bf16[1536,3072]{1,0:T(8,128)(2,1)} %param.11, s32[]{:T(128)S(6)} %select_n.56, s32[]{:T(128)S(6)} %select_n.55, ...), kind=kLoop, calls=%fused_computation.133 | loop fusion | bytes 4718624 | tf_op jit(solution)/shard_map/dynamic_slice | solution.py:294
  14.6 3.2 %fusion.50 = (bf16[256,1536]{1,0:T(8,128)(2,1)S(1)}, bf16[256,1536]{1,0:T(8,128)(2,1)S(1)}, bf16[256,1536]{1,0:T(8,128)(2,1)S(1)}, bf16[256,1536]{1,0:T(8,128)(2...) fusion(bf16[1536,3072]{1,0:T(8,128)(2,1)} %param.11, ...), kind=kLoop, calls=%fused_computation.134 | loop fusion | bytes 12582936 | tf_op jit(solution)/shard_map/dynamic_slice | solution.py:294
  18.0 1.8 %pad_maximum_fusion = bf16[1024,1536]{1,0:T(8,128)(2,1)} fusion(bf16[256,1536]{1,0:T(8,128)(2,1)S(1)} %get-tuple-element.99, bf16[256,1536]{1,0:T(8,128)(2,1)S(1)} %get-tuple-element.100, bf16[256,1536]{1,0:T(8,128)(2,1)S(1)} %get-tuple-element.101, bf16[256,1536]{1,0:T(8,128)(2,1)S(1)} %get-tuple-element.102), kind=kLoop, calls=%fused_computation | loop fusion | flops 12582912 | bytes 6291456 | tf_op jit(solution)/shard_map/concatenate | solution.py:305
  22.2 21.7 %collective-permute-done.refs_1_ = bf16[3,336,256]{2,1,0:T(8,128)(2,1)S(1)} collective-permute-done((bf16[3,336,256]{2,1,0:T(8,128)(2,1)}, bf16[3,336,256]{2,1,0:T(8,128)(2,1)S(1)}, u32[]{:S(2)}, u32[]{:S(2)}) %collective-permute-start) | collective-permute-done | bytes 516128 | tf_op jit(solution)/shard_map/ppermute | solution.py:259
  44.1 1.6 %collective-permute-start.3 = (bf16[2,2,320,256]{3,2,1,0:T(8,128)(2,1)S(1)}, bf16[2,2,320,256]{3,2,1,0:T(8,128)(2,1)S(1)}, u32[]{:S(2)}, u32[]{:S(2)}) collective-permute-start(bf16[2,2,320,256]{3,2,1,0:T(8,128)(2,1)S(1)} %pad_maximum_fusion.4.refs_4_), channel_id=1, source_target_pairs={{0,4},{2,6},{4,0},{6,2},{8,12},{10,14},{12,8},{14,10},{16,20},{18,... | collective-permute-start | bytes 1966088 | tf_op jit(solution)/shard_map/ppermute | solution.py:259
  47.2 14.1 %collective-permute-done.3.refs_4_ = bf16[2,2,320,256]{3,2,1,0:T(8,128)(2,1)S(1)} collective-permute-done((bf16[2,2,320,256]{3,2,1,0:T(8,128)(2,1)S(1)}, bf16[2,2,320,256]{3,2,1,0:T(8,128)(2,1)S(1)}, u32[]{:S(2)}, u32[]{:S(2)}) %collective-permute-start.3) | collective-permute-done | bytes 655392 | tf_op jit(solution)/shard_map/ppermute | solution.py:259
  64.5 3.6 %collective-permute-start.7 = (bf16[3,336,128]{2,1,0:T(8,128)(2,1)S(1)}, bf16[3,336,128]{2,1,0:T(8,128)(2,1)S(1)}, u32[]{:S(2)}, u32[]{:S(2)}) collective-permute-start(bf16[3,336,128]{2,1,0:T(8,128)(2,1)S(1)} %get-tuple-element.51), channel_id=1, source_target_pairs={{0,16},{2,18},{4,20},{6,22},{8,24},{10,26},{12,28},{14,30},{16,0},... | collective-permute-start | bytes 774152 | tf_op jit(solution)/shard_map/ppermute | solution.py:259
  69.1 10.2 %attend_slots.4 = (f32[4,2,1,320]{3,2,1,0:T(1,128)S(1)}, f32[4,2,1,320]{3,2,1,0:T(1,128)S(1)}, f32[4,2,128,320]{3,2,1,0:T(8,128)S(1)}) custom-call(s32[4,8]{1,0:T(4,128)S(1)} %get-tuple-element.127.flags_ref, bf16[3,336,256]{2,1,0:T(8,128)(2,1)S(1)} %get-tuple-element.136.refs_0_, bf16[3,336,256]{2,1,0:T(8,128)(2,1)S(1)} %collective-permute-done.refs_1_, ...), custom_call_target="tpu_custom_call" | custom-call | tf_op jit(solution)/shard_map/attend_slots/pallas_call | solution.py:223
  79.3 7.0 %collective-permute-done.7.refs_2_ = bf16[3,336,128]{2,1,0:T(8,128)(2,1)S(1)} collective-permute-done((bf16[3,336,128]{2,1,0:T(8,128)(2,1)S(1)}, bf16[3,336,128]{2,1,0:T(8,128)(2,1)S(1)}, u32[]{:S(2)}, u32[]{:S(2)}) %collective-permute-start.7) | collective-permute-done | bytes 258080 | tf_op jit(solution)/shard_map/ppermute | solution.py:259
  89.1 14.5 %attend_slots.5 = (bf16[320,256]{1,0:T(8,128)(2,1)S(1)}, bf16[320,256]{1,0:T(8,128)(2,1)S(1)}, bf16[320,256]{1,0:T(8,128)(2,1)S(1)}, bf16[320,256]{1,0:T(8,128)(2,1)S(1)}) custom-call(s32[4,8]{1,0:T(4,128)S(1)} %get-tuple-element.128.flags_ref, bf16[3,336,256]{2,1,0:T(8,128)(2,1)S(1)} %get-tuple-element.136.refs_0_, ...), custom_call_target="tpu_custom_call" | custom-call | tf_op jit(solution)/shard_map/attend_slots/pallas_call | solution.py:223
  103.6 2.8 %collective-permute-start.20 = (bf16[320,256]{1,0:T(8,128)(2,1)S(1)}, bf16[320,256]{1,0:T(8,128)(2,1)S(1)}, u32[]{:S(2)}, u32[]{:S(2)}) collective-permute-start(bf16[320,256]{1,0:T(8,128)(2,1)S(1)} %get-tuple-element.65), channel_id=1, source_target_pairs={{0,24},{2,26},{4,28},{6,30},{8,16},{10,18},{12,20},{14,22},{16,8},... | collective-permute-start | bytes 491528 | tf_op jit(solution)/shard_map/ppermute | solution.py:259
  106.4 4.1 %collective-permute-start.19 = (bf16[320,256]{1,0:T(8,128)(2,1)S(1)}, bf16[320,256]{1,0:T(8,128)(2,1)S(1)}, u32[]{:S(2)}, u32[]{:S(2)}) collective-permute-start(bf16[320,256]{1,0:T(8,128)(2,1)S(1)} %get-tuple-element.64), channel_id=1, source_target_pairs={{0,16},{2,18},{4,20},{6,22},{8,24},{10,26},{12,28},{14,30},{16,0},... | collective-permute-start | bytes 491528 | tf_op jit(solution)/shard_map/ppermute | solution.py:259
  110.5 2.2 %collective-permute-start.16 = (bf16[2,2,320,128]{3,2,1,0:T(8,128)(2,1)S(1)}, bf16[2,2,320,128]{3,2,1,0:T(8,128)(2,1)S(1)}, u32[]{:S(2)}, u32[]{:S(2)}) collective-permute-start(bf16[2,2,320,128]{3,2,1,0:T(8,128)(2,1)S(1)} %collective-permute-done.14.refs_4_), channel_id=1, source_target_pairs={{0,2},{2,0},{4,6},{6,4},{8,10},{10,8},{12,14},{14,12},{16,18},{18,... | collective-permute-start | bytes 983048 | tf_op jit(solution)/shard_map/ppermute | solution.py:259
  112.9 7.5 %attend_slots.6 = (f32[4,1,1,320]{3,2,1,0:T(1,128)S(1)}, f32[4,1,1,320]{3,2,1,0:T(1,128)S(1)}, f32[4,1,128,320]{3,2,1,0:T(8,128)S(1)}) custom-call(s32[4,8]{1,0:T(4,128)S(1)} %get-tuple-element.127.flags_ref, bf16[3,336,128]{2,1,0:T(8,128)(2,1)S(1)} %get-tuple-element.66.refs_0_, bf16[3,336,128]{2,1,0:T(8,128)(2,1)S(1)} %collective-permute-done.6.refs_1_, ...), custom_call_target="tpu_custom_call" | custom-call | tf_op jit(solution)/shard_map/attend_slots/pallas_call | solution.py:223
  122.0 2.1 %convolution_convert_fusion = bf16[320,1536]{1,0:T(8,128)(2,1)} fusion(bf16[320,1024]{1,0:T(8,128)(2,1)S(1)} %pad_maximum_fusion.6, bf16[1024,1536]{1,0:T(8,128)(2,1)S(1)} %pad_maximum_fusion.1), kind=kOutput, calls=%fused_computation.5 | convolution fusion | flops 1007124480 | bytes 4784128 | tf_op jit(solution)/shard_map/dot_general | solution.py:348
  125.6 9.4 %attend_slots.7 = (bf16[320,128]{1,0:T(8,128)(2,1)S(1)}, bf16[320,128]{1,0:T(8,128)(2,1)S(1)}, bf16[320,128]{1,0:T(8,128)(2,1)S(1)}, bf16[320,128]{1,0:T(8,128)(2,1)S(1)}) custom-call(s32[4,8]{1,0:T(4,128)S(1)} %get-tuple-element.128.flags_ref, bf16[3,336,128]{2,1,0:T(8,128)(2,1)S(1)} %get-tuple-element.66.refs_0_, ...), custom_call_target="tpu_custom_call" | custom-call | tf_op jit(solution)/shard_map/attend_slots/pallas_call | solution.py:223
  136.0 3.4 %collective-permute-start.24 = (bf16[320,128]{1,0:T(8,128)(2,1)S(1)}, bf16[320,128]{1,0:T(8,128)(2,1)S(1)}, u32[]{:S(2)}, u32[]{:S(2)}) collective-permute-start(bf16[320,128]{1,0:T(8,128)(2,1)S(1)} %get-tuple-element.78), channel_id=1, source_target_pairs={{0,16},{2,18},{4,20},{6,22},{8,24},{10,26},{12,28},{14,30},{16,0},... | collective-permute-start | bytes 245768 | tf_op jit(solution)/shard_map/ppermute | solution.py:259
  139.6 2.4 %fusion.52 = f32[320,1536]{1,0:T(8,128)S(1)} fusion(bf16[320,1024]{1,0:T(8,128)(2,1)} %copy-done.3, bf16[1024,1536]{1,0:T(8,128)(2,1)S(1)} %copy-done), kind=kOutput, calls=%fused_computation.136 | convolution fusion | flops 1006632960 | bytes 5767168 | tf_op jit(solution)/shard_map/dot_general | solution.py:348
  142.1 2.0 %collective-permute-done.24 = bf16[320,128]{1,0:T(8,128)(2,1)S(1)} collective-permute-done((bf16[320,128]{1,0:T(8,128)(2,1)S(1)}, bf16[320,128]{1,0:T(8,128)(2,1)S(1)}, u32[]{:S(2)}, u32[]{:S(2)}) %collective-permute-start.24) | collective-permute-done | bytes 81952 | tf_op jit(solution)/shard_map/ppermute | solution.py:259
  144.1 2.5 %collective-permute-done.25 = bf16[320,128]{1,0:T(8,128)(2,1)S(1)} collective-permute-done((bf16[320,128]{1,0:T(8,128)(2,1)S(1)}, bf16[320,128]{1,0:T(8,128)(2,1)S(1)}, u32[]{:S(2)}, u32[]{:S(2)}) %collective-permute-start.25) | collective-permute-done | bytes 81952 | tf_op jit(solution)/shard_map/ppermute | solution.py:259
  147.2 1.7 %collective-permute-done.27 = bf16[320,1536]{1,0:T(8,128)(2,1)} collective-permute-done((bf16[320,1536]{1,0:T(8,128)(2,1)}, bf16[320,1536]{1,0:T(8,128)(2,1)}, u32[]{:S(2)}, u32[]{:S(2)}) %collective-permute-start.27) | collective-permute-done | bytes 983072 | tf_op jit(solution)/shard_map/ppermute | solution.py:265
  149.0 1.9 %fusion = f32[320,1536]{1,0:T(8,128)S(1)} fusion(f32[320,1536]{1,0:T(8,128)S(1)} %fusion.52, bf16[320,512]{1,0:T(8,128)(2,1)S(1)} %constant_dynamic-update-slice_fusion, bf16[320,1536]{1,0:T(8,128)(2,1)} %collective-permute-done.27, bf16[128,1536]{1,0:T(8,128)(2,1)S(1)} %copy-done.5, bf16[128,1536]{1,0:T(8,128)(2,1)S(1)} %copy-done.6, ...), kind=kOutput, calls=%fused_computation.4 | convolution fusion | flops 511082496 | bytes 6815744 | tf_op jit(solution)/shard_map/dot_general | solution.py:348
  150.9 5.4 %collective-permute-done.26 = bf16[320,512]{1,0:T(8,128)(2,1)S(1)} collective-permute-done((bf16[320,512]{1,0:T(8,128)(2,1)S(1)}, bf16[320,512]{1,0:T(8,128)(2,1)S(1)}, u32[]{:S(2)}, u32[]{:S(2)}) %collective-permute-start.26) | collective-permute-done | bytes 327712 | tf_op jit(solution)/shard_map/ppermute | solution.py:265
  (102 shorter events, 26.6 us)
Async XLA Ops:
  4.5 42.7 %collective-permute-start.1 = (bf16[3,336,256]{2,1,0:T(8,128)(2,1)}, bf16[3,336,256]{2,1,0:T(8,128)(2,1)S(1)}, u32[]{:S(2)}, u32[]{:S(2)}) collective-permute-start(bf16[3,336,256]{2,1,0:T(8,128)(2,1)} %get-tuple-element.135), channel_id=1, source_target_pairs={{0,16},{2,18},{4,20},{6,22},{8,24},{10,26},{12,28},{14,30},{16,0},... | collective-permute-start | bytes 1548296 | tf_op jit(solution)/shard_map/ppermute | solution.py:259
  8.5 38.7 %collective-permute-start.2 = (bf16[3,336,256]{2,1,0:T(8,128)(2,1)S(1)}, bf16[3,336,256]{2,1,0:T(8,128)(2,1)S(1)}, u32[]{:S(2)}, u32[]{:S(2)}) collective-permute-start(bf16[3,336,256]{2,1,0:T(8,128)(2,1)S(1)} %get-tuple-element.133), channel_id=1, source_target_pairs={{0,24},{2,26},{4,28},{6,30},{8,16},{10,18},{12,20},{14,22},{16,8},... | collective-permute-start | bytes 1548296 | tf_op jit(solution)/shard_map/ppermute | solution.py:259
  9.9 34.1 %collective-permute-start = (bf16[3,336,256]{2,1,0:T(8,128)(2,1)}, bf16[3,336,256]{2,1,0:T(8,128)(2,1)S(1)}, u32[]{:S(2)}, u32[]{:S(2)}) collective-permute-start(bf16[3,336,256]{2,1,0:T(8,128)(2,1)} %get-tuple-element.134), channel_id=1, source_target_pairs={{0,8},{2,10},{4,12},{6,14},{8,0},{10,2},{12,4},{14,6},{16,24},{18,... | collective-permute-start | bytes 1548296 | tf_op jit(solution)/shard_map/ppermute | solution.py:259
  13.0 31.0 %collective-permute-start.4 = (bf16[256,1536]{1,0:T(8,128)(2,1)S(1)}, bf16[256,1536]{1,0:T(8,128)(2,1)}, u32[]{:S(2)}, u32[]{:S(2)}) collective-permute-start(bf16[256,1536]{1,0:T(8,128)(2,1)S(1)} %pad_maximum_fusion.3), channel_id=1, source_target_pairs={{0,1},{1,0},{2,3},{3,2},{4,5},{5,4},{6,7},{7,6},{8,9},{9,8},{10,11... | collective-permute-start | bytes 2359304 | tf_op jit(solution)/shard_map/ppermute | solution.py:265
  44.0 17.3 %collective-permute-start.5 = (bf16[256,1536]{1,0:T(8,128)(2,1)}, bf16[256,1536]{1,0:T(8,128)(2,1)S(1)}, u32[]{:S(2)}, u32[]{:S(2)}) collective-permute-start(bf16[256,1536]{1,0:T(8,128)(2,1)} %collective-permute-done.4), channel_id=1, source_target_pairs={{0,2},{2,0},{4,6},{6,4},{8,10},{10,8},{12,14},{14,12},{16,18},{18,... | collective-permute-start | bytes 2359304 | tf_op jit(solution)/shard_map/ppermute | solution.py:259
  44.1 17.2 %collective-permute-start.3 = (bf16[2,2,320,256]{3,2,1,0:T(8,128)(2,1)S(1)}, bf16[2,2,320,256]{3,2,1,0:T(8,128)(2,1)S(1)}, u32[]{:S(2)}, u32[]{:S(2)}) collective-permute-start(bf16[2,2,320,256]{3,2,1,0:T(8,128)(2,1)S(1)} %pad_maximum_fusion.4.refs_4_), channel_id=1, source_target_pairs={{0,4},{2,6},{4,0},{6,2},{8,12},{10,14},{12,8},{14,10},{16,20},{18,... | collective-permute-start | bytes 1966088 | tf_op jit(solution)/shard_map/ppermute | solution.py:259
  46.9 21.5 %collective-permute-start.9 = (bf16[2,2,320,256]{3,2,1,0:T(8,128)(2,1)S(1)}, bf16[2,2,320,256]{3,2,1,0:T(8,128)(2,1)S(1)}, u32[]{:S(2)}, u32[]{:S(2)}) collective-permute-start(bf16[2,2,320,256]{3,2,1,0:T(8,128)(2,1)S(1)} %pad_maximum_fusion.4.refs_4_), channel_id=1, source_target_pairs={{0,2},{2,0},{4,6},{6,4},{8,10},{10,8},{12,14},{14,12},{16,18},{18,... | collective-permute-start | bytes 1966088 | tf_op jit(solution)/shard_map/ppermute | solution.py:259
  62.5 24.5 %collective-permute-start.11 = (bf16[2,2,320,256]{3,2,1,0:T(8,128)(2,1)S(1)}, bf16[2,2,320,256]{3,2,1,0:T(8,128)(2,1)S(1)}, u32[]{:S(2)}, u32[]{:S(2)}) collective-permute-start(bf16[2,2,320,256]{3,2,1,0:T(8,128)(2,1)S(1)} %pad_maximum_fusion.5.refs_5_), channel_id=1, source_target_pairs={{0,4},{2,6},{4,0},{6,2},{8,12},{10,14},{12,8},{14,10},{16,20},{18,... | collective-permute-start | bytes 1966088 | tf_op jit(solution)/shard_map/ppermute | solution.py:259
  64.1 15.2 %collective-permute-start.6 = (bf16[3,336,128]{2,1,0:T(8,128)(2,1)S(1)}, bf16[3,336,128]{2,1,0:T(8,128)(2,1)S(1)}, u32[]{:S(2)}, u32[]{:S(2)}) collective-permute-start(bf16[3,336,128]{2,1,0:T(8,128)(2,1)S(1)} %get-tuple-element.50), channel_id=1, source_target_pairs={{0,8},{2,10},{4,12},{6,14},{8,0},{10,2},{12,4},{14,6},{16,24},{18,... | collective-permute-start | bytes 774152 | tf_op jit(solution)/shard_map/ppermute | solution.py:259
  64.5 21.8 %collective-permute-start.7 = (bf16[3,336,128]{2,1,0:T(8,128)(2,1)S(1)}, bf16[3,336,128]{2,1,0:T(8,128)(2,1)S(1)}, u32[]{:S(2)}, u32[]{:S(2)}) collective-permute-start(bf16[3,336,128]{2,1,0:T(8,128)(2,1)S(1)} %get-tuple-element.51), channel_id=1, source_target_pairs={{0,16},{2,18},{4,20},{6,22},{8,24},{10,26},{12,28},{14,30},{16,0},... | collective-permute-start | bytes 774152 | tf_op jit(solution)/shard_map/ppermute | solution.py:259
  68.5 17.9 %collective-permute-start.8 = (bf16[3,336,128]{2,1,0:T(8,128)(2,1)S(1)}, bf16[3,336,128]{2,1,0:T(8,128)(2,1)S(1)}, u32[]{:S(2)}, u32[]{:S(2)}) collective-permute-start(bf16[3,336,128]{2,1,0:T(8,128)(2,1)S(1)} %get-tuple-element.52), channel_id=1, source_target_pairs={{0,24},{2,26},{4,28},{6,30},{8,16},{10,18},{12,20},{14,22},{16,8},... | collective-permute-start | bytes 774152 | tf_op jit(solution)/shard_map/ppermute | solution.py:259
  69.0 19.8 %collective-permute-start.12 = (bf16[2,2,320,256]{3,2,1,0:T(8,128)(2,1)S(1)}, bf16[2,2,320,256]{3,2,1,0:T(8,128)(2,1)S(1)}, u32[]{:S(2)}, u32[]{:S(2)}) collective-permute-start(bf16[2,2,320,256]{3,2,1,0:T(8,128)(2,1)S(1)} %collective-permute-done.3.refs_4_), channel_id=1, source_target_pairs={{0,2},{2,0},{4,6},{6,4},{8,10},{10,8},{12,14},{14,12},{16,18},{18,... | collective-permute-start | bytes 1966088 | tf_op jit(solution)/shard_map/ppermute | solution.py:259
  86.4 20.0 %collective-permute-start.14 = (bf16[2,2,320,128]{3,2,1,0:T(8,128)(2,1)S(1)}, bf16[2,2,320,128]{3,2,1,0:T(8,128)(2,1)S(1)}, u32[]{:S(2)}, u32[]{:S(2)}) collective-permute-start(bf16[2,2,320,128]{3,2,1,0:T(8,128)(2,1)S(1)} %pad_maximum_fusion.7.refs_4_), channel_id=1, source_target_pairs={{0,4},{2,6},{4,0},{6,2},{8,12},{10,14},{12,8},{14,10},{16,20},{18,... | collective-permute-start | bytes 983048 | tf_op jit(solution)/shard_map/ppermute | solution.py:259
  87.0 23.4 %collective-permute-start.15 = (bf16[2,2,320,128]{3,2,1,0:T(8,128)(2,1)S(1)}, bf16[2,2,320,128]{3,2,1,0:T(8,128)(2,1)}, u32[]{:S(2)}, u32[]{:S(2)}) collective-permute-start(bf16[2,2,320,128]{3,2,1,0:T(8,128)(2,1)S(1)} %pad_maximum_fusion.8.refs_5_), channel_id=1, source_target_pairs={{0,4},{2,6},{4,0},{6,2},{8,12},{10,14},{12,8},{14,10},{16,20},{18,... | collective-permute-start | bytes 983048 | tf_op jit(solution)/shard_map/ppermute | solution.py:259
  88.6 21.9 %collective-permute-start.21 = (bf16[2,2,320,128]{3,2,1,0:T(8,128)(2,1)S(1)}, bf16[2,2,320,128]{3,2,1,0:T(8,128)(2,1)S(1)}, u32[]{:S(2)}, u32[]{:S(2)}) collective-permute-start(bf16[2,2,320,128]{3,2,1,0:T(8,128)(2,1)S(1)} %pad_maximum_fusion.7.refs_4_), channel_id=1, source_target_pairs={{0,2},{2,0},{4,6},{6,4},{8,10},{10,8},{12,14},{14,12},{16,18},{18,... | collective-permute-start | bytes 983048 | tf_op jit(solution)/shard_map/ppermute | solution.py:259
  88.9 23.9 %collective-permute-start.22 = (bf16[2,2,320,128]{3,2,1,0:T(8,128)(2,1)S(1)}, bf16[2,2,320,128]{3,2,1,0:T(8,128)(2,1)S(1)}, u32[]{:S(2)}, u32[]{:S(2)}) collective-permute-start(bf16[2,2,320,128]{3,2,1,0:T(8,128)(2,1)S(1)} %pad_maximum_fusion.8.refs_5_), channel_id=1, source_target_pairs={{0,2},{2,0},{4,6},{6,4},{8,10},{10,8},{12,14},{14,12},{16,18},{18,... | collective-permute-start | bytes 983048 | tf_op jit(solution)/shard_map/ppermute | solution.py:259
  103.6 16.8 %collective-permute-start.20 = (bf16[320,256]{1,0:T(8,128)(2,1)S(1)}, bf16[320,256]{1,0:T(8,128)(2,1)S(1)}, u32[]{:S(2)}, u32[]{:S(2)}) collective-permute-start(bf16[320,256]{1,0:T(8,128)(2,1)S(1)} %get-tuple-element.65), channel_id=1, source_target_pairs={{0,24},{2,26},{4,28},{6,30},{8,16},{10,18},{12,20},{14,22},{16,8},... | collective-permute-start | bytes 491528 | tf_op jit(solution)/shard_map/ppermute | solution.py:259
  106.4 15.5 %collective-permute-start.19 = (bf16[320,256]{1,0:T(8,128)(2,1)S(1)}, bf16[320,256]{1,0:T(8,128)(2,1)S(1)}, u32[]{:S(2)}, u32[]{:S(2)}) collective-permute-start(bf16[320,256]{1,0:T(8,128)(2,1)S(1)} %get-tuple-element.64), channel_id=1, source_target_pairs={{0,16},{2,18},{4,20},{6,22},{8,24},{10,26},{12,28},{14,30},{16,0},... | collective-permute-start | bytes 491528 | tf_op jit(solution)/shard_map/ppermute | solution.py:259
  110.5 11.4 %collective-permute-start.18 = (bf16[320,256]{1,0:T(8,128)(2,1)S(1)}, bf16[320,256]{1,0:T(8,128)(2,1)S(1)}, u32[]{:S(2)}, u32[]{:S(2)}) collective-permute-start(bf16[320,256]{1,0:T(8,128)(2,1)S(1)} %get-tuple-element.63), channel_id=1, source_target_pairs={{0,8},{2,10},{4,12},{6,14},{8,0},{10,2},{12,4},{14,6},{16,24},{18,... | collective-permute-start | bytes 491528 | tf_op jit(solution)/shard_map/ppermute | solution.py:259
  110.5 15.1 %collective-permute-start.16 = (bf16[2,2,320,128]{3,2,1,0:T(8,128)(2,1)S(1)}, bf16[2,2,320,128]{3,2,1,0:T(8,128)(2,1)S(1)}, u32[]{:S(2)}, u32[]{:S(2)}) collective-permute-start(bf16[2,2,320,128]{3,2,1,0:T(8,128)(2,1)S(1)} %collective-permute-done.14.refs_4_), channel_id=1, source_target_pairs={{0,2},{2,0},{4,6},{6,4},{8,10},{10,8},{12,14},{14,12},{16,18},{18,... | collective-permute-start | bytes 983048 | tf_op jit(solution)/shard_map/ppermute | solution.py:259
  112.8 12.8 %collective-permute-start.17 = (bf16[2,2,320,128]{3,2,1,0:T(8,128)(2,1)}, bf16[2,2,320,128]{3,2,1,0:T(8,128)(2,1)S(1)}, u32[]{:S(2)}, u32[]{:S(2)}) collective-permute-start(bf16[2,2,320,128]{3,2,1,0:T(8,128)(2,1)} %collective-permute-done.15.refs_5_), channel_id=1, source_target_pairs={{0,2},{2,0},{4,6},{6,4},{8,10},{10,8},{12,14},{14,12},{16,18},{18,... | collective-permute-start | bytes 983048 | tf_op jit(solution)/shard_map/ppermute | solution.py:259
  124.1 24.8 %collective-permute-start.27 = (bf16[320,1536]{1,0:T(8,128)(2,1)}, bf16[320,1536]{1,0:T(8,128)(2,1)}, u32[]{:S(2)}, u32[]{:S(2)}) collective-permute-start(bf16[320,1536]{1,0:T(8,128)(2,1)} %convolution_convert_fusion), channel_id=1, source_target_pairs={{0,1},{1,0},{2,3},{3,2},{4,5},{5,4},{6,7},{7,6},{8,9},{9,8},{10,11... | collective-permute-start | bytes 2949128 | tf_op jit(solution)/shard_map/ppermute | solution.py:265
  136.0 8.0 %collective-permute-start.24 = (bf16[320,128]{1,0:T(8,128)(2,1)S(1)}, bf16[320,128]{1,0:T(8,128)(2,1)S(1)}, u32[]{:S(2)}, u32[]{:S(2)}) collective-permute-start(bf16[320,128]{1,0:T(8,128)(2,1)S(1)} %get-tuple-element.78), channel_id=1, source_target_pairs={{0,16},{2,18},{4,20},{6,22},{8,24},{10,26},{12,28},{14,30},{16,0},... | collective-permute-start | bytes 245768 | tf_op jit(solution)/shard_map/ppermute | solution.py:259
  146.6 9.6 %collective-permute-start.26 = (bf16[320,512]{1,0:T(8,128)(2,1)S(1)}, bf16[320,512]{1,0:T(8,128)(2,1)S(1)}, u32[]{:S(2)}, u32[]{:S(2)}) collective-permute-start(bf16[320,512]{1,0:T(8,128)(2,1)S(1)} %constant_dynamic-update-slice_fusion), channel_id=1, source_target_pairs={{0,1},{1,0},{2,3},{3,2},{4,5},{5,4},{6,7},{7,6},{8,9},{9,8},{10,11... | collective-permute-start | bytes 983048 | tf_op jit(solution)/shard_map/ppermute | solution.py:265
  (13 other events, 88.6 us)

commit v3 on v2

--- a/solution.py
+++ b/solution.py
@@ -276,13 +276,15 @@
             ((0, 2), (rows, PAT_ROWS - 1), (0, heads * HD - 2 * REACH)),
         )
         pieces = []
-        for k in range(PLANES):
+        for k in (1, 2, 3, 0):
+            if k == 2:
+                arrays = after(arrays, pieces)
             first = ((plane ^ k) * per_plane + start) * HD
             piece = jnp.stack(
                 [lax.dynamic_slice_in_dim(array, first, heads * HD, 1) for array in arrays]
             )
             pieces.append(jnp.pad(piece, ((0, 0), (0, PAT_ROWS), (0, 0))) + note)
-        return pieces
+        return [pieces[3]] + pieces[:3]
 
     arrays = (key_rows, value_rows, query_rows)
     half = width // 2

time: 159 us -> 154 us (0.969)
  waiting for transfers between devices: 56 us -> 42 us
  Pallas kernels: 41.7 us -> 45.7 us
  other arithmetic: 4.8 us -> 6.68 us
    ppermute x25, waiting for transfers between devices: 48.9 us -> 29.3 us  [swap(): return lax.ppermute(value, 'seq', [(i, i ^ bits) for i in range(blocks)])]
    ppermute x3, waiting for transfers between devices: 7.11 us -> 12.7 us  [across(): return lax.ppermute(value, 'head', [(0, 1), (1, 0)])]
    pallas_call x4, Pallas kernels: 41.7 us -> 45.7 us  [attend(): pl.pallas_call(functools.partial(attend_kernel, heads, plan, not state, l...]
    another operation x5 -> x11, local copies, waits for them, and re-layouts: 5.83 us -> 6.98 us  [pack_heads(): jnp.stack([lax.dynamic_slice_in_dim(array, first, heads * HD, 1) for arra...]
  transfers between devices with their start and end apart: 28 -> 28, of which waited for: 8 -> 10; matrix products, arithmetic and copies ran while one was open for 12% -> 15% of each run, Pallas kernels for 26% -> 30%
where the time goes in v3:
time: 154 us
  Pallas kernels  45.7 us (30%)
  waiting for transfers between devices  42 us (27%)
  starting transfers between devices  35.4 us (23%)
  local copies, waits for them, and re-layouts  14.3 us (9%)
  matrix products  9.31 us (6%)
  other arithmetic  6.68 us (4%)
    pallas_call x4, Pallas kernels, attend(): pl.pallas_call(functools.partial(attend_kernel, heads, plan, not state, l...  45.7 us
    ppermute x25, starting transfers between devices, swap(): return lax.ppermute(value, 'seq', [(i, i ^ bits) for i in range(blocks)])  31.6 us
    ppermute x25, waiting for transfers between devices, swap(): return lax.ppermute(value, 'seq', [(i, i ^ bits) for i in range(blocks)])  29.3 us
    ppermute x3, waiting for transfers between devices, across(): return lax.ppermute(value, 'head', [(0, 1), (1, 0)])  12.7 us
    another operation x11, local copies, waits for them, and re-layouts, pack_heads(): jnp.stack([lax.dynamic_slice_in_dim(array, first, heads * HD, 1) for arra...  6.98 us
    dot_general x3, matrix products, project(): jnp.dot(near, weight_sides[at][c], preferred_element_type=F32)  6.27 us
    dynamic_slice x2, local copies, waits for them, and re-layouts, weight_rows(): lax.dynamic_slice(weight, (((plane ^ k) * per_plane + starts[c]) * HD, si...  6.07 us
    ppermute x3, starting transfers between devices, across(): return lax.ppermute(value, 'head', [(0, 1), (1, 0)])  3.79 us
  transfers between devices with their start and end apart: 28, of which 10 were waited for; matrix products, arithmetic and copies ran while one was open for 15% of the time, Pallas kernels for 30%

profile of v3, /device:TPU:0, one launch (start us, length us, event | category | flops | bytes accessed | tf_op | source)
XLA Modules:
  0.0 153.8 jit_solution(14822810740850423661)
XLA Ops:
  3.6 3.0 %collective-permute-start = (bf16[3,336,256]{2,1,0:T(8,128)(2,1)}, bf16[3,336,256]{2,1,0:T(8,128)(2,1)S(1)}, u32[]{:S(2)}, u32[]{:S(2)}) collective-permute-start(bf16[3,336,256]{2,1,0:T(8,128)(2,1)} %pad_add_fusion.3), channel_id=1, source_target_pairs={{0,8},{2,10},{4,12},{6,14},{8,0},{10,2},{12,4},{14,6},{16,24},{18,... | collective-permute-start | bytes 1548296 | tf_op jit(solution)/shard_map/ppermute | solution.py:259
  9.0 2.6 %collective-permute-start.1 = (bf16[3,336,256]{2,1,0:T(8,128)(2,1)}, bf16[3,336,256]{2,1,0:T(8,128)(2,1)S(1)}, u32[]{:S(2)}, u32[]{:S(2)}) collective-permute-start(bf16[3,336,256]{2,1,0:T(8,128)(2,1)} %get-tuple-element.140), channel_id=1, source_target_pairs={{0,16},{2,18},{4,20},{6,22},{8,24},{10,26},{12,28},{14,30},{16,0},... | collective-permute-start | bytes 1548296 | tf_op jit(solution)/shard_map/ppermute | solution.py:259
  11.6 2.9 %fusion.49 = (bf16[128,1536]{1,0:T(8,128)(2,1)}, bf16[128,1536]{1,0:T(8,128)(2,1)S(1)}, bf16[128,1536]{1,0:T(8,128)(2,1)S(1)}, bf16[128,1536]{1,0:T(8,128)(2,1)}...) fusion(bf16[1536,3072]{1,0:T(8,128)(2,1)} %param.11, s32[]{:T(128)S(6)} %select_n.56, s32[]{:T(128)S(6)} %select_n.55, ...), kind=kLoop, calls=%fused_computation.133 | loop fusion | bytes 4718624 | tf_op jit(solution)/shard_map/dynamic_slice | solution.py:296
  15.4 1.7 %collective-permute-start.4 = (bf16[256,1536]{1,0:T(8,128)(2,1)}, bf16[256,1536]{1,0:T(8,128)(2,1)}, u32[]{:S(2)}, u32[]{:S(2)}) collective-permute-start(bf16[256,1536]{1,0:T(8,128)(2,1)} %pad_maximum_fusion.3), channel_id=1, source_target_pairs={{0,1},{1,0},{2,3},{3,2},{4,5},{5,4},{6,7},{7,6},{8,9},{9,8},{10,11... | collective-permute-start | bytes 2359304 | tf_op jit(solution)/shard_map/ppermute | solution.py:265
  17.1 3.2 %fusion.50 = (bf16[256,1536]{1,0:T(8,128)(2,1)S(1)}, bf16[256,1536]{1,0:T(8,128)(2,1)S(1)}, bf16[256,1536]{1,0:T(8,128)(2,1)S(1)}, bf16[256,1536]{1,0:T(8,128)(2...) fusion(bf16[1536,3072]{1,0:T(8,128)(2,1)} %param.11, ...), kind=kLoop, calls=%fused_computation.134 | loop fusion | bytes 12582936 | tf_op jit(solution)/shard_map/dynamic_slice | solution.py:296
  22.4 1.8 %pad_maximum_fusion = bf16[1024,1536]{1,0:T(8,128)(2,1)} fusion(bf16[256,1536]{1,0:T(8,128)(2,1)S(1)} %get-tuple-element.111, bf16[256,1536]{1,0:T(8,128)(2,1)S(1)} %get-tuple-element.112, bf16[256,1536]{1,0:T(8,128)(2,1)S(1)} %get-tuple-element.113, bf16[256,1536]{1,0:T(8,128)(2,1)S(1)} %get-tuple-element.114), kind=kLoop, calls=%fused_computation | loop fusion | flops 12582912 | bytes 6291456 | tf_op jit(solution)/shard_map/concatenate | solution.py:307
  27.2 7.2 %collective-permute-done.4 = bf16[256,1536]{1,0:T(8,128)(2,1)} collective-permute-done((bf16[256,1536]{1,0:T(8,128)(2,1)}, bf16[256,1536]{1,0:T(8,128)(2,1)}, u32[]{:S(2)}, u32[]{:S(2)}) %collective-permute-start.4) | collective-permute-done | bytes 786464 | tf_op jit(solution)/shard_map/ppermute | solution.py:265
  34.5 1.6 %collective-permute-start.3 = (bf16[2,2,320,256]{3,2,1,0:T(8,128)(2,1)S(1)}, bf16[2,2,320,256]{3,2,1,0:T(8,128)(2,1)S(1)}, u32[]{:S(2)}, u32[]{:S(2)}) collective-permute-start(bf16[2,2,320,256]{3,2,1,0:T(8,128)(2,1)S(1)} %pad_maximum_fusion.4.refs_4_), channel_id=1, source_target_pairs={{0,4},{2,6},{4,0},{6,2},{8,12},{10,14},{12,8},{14,10},{16,20},{18,... | collective-permute-start | bytes 1966088 | tf_op jit(solution)/shard_map/ppermute | solution.py:259
  36.5 10.4 %collective-permute-done.1.refs_2_ = bf16[3,336,256]{2,1,0:T(8,128)(2,1)S(1)} collective-permute-done((bf16[3,336,256]{2,1,0:T(8,128)(2,1)}, bf16[3,336,256]{2,1,0:T(8,128)(2,1)S(1)}, u32[]{:S(2)}, u32[]{:S(2)}) %collective-permute-start.1) | collective-permute-done | bytes 516128 | tf_op jit(solution)/shard_map/ppermute | solution.py:259
  46.9 4.8 %collective-permute-done.3.refs_4_ = bf16[2,2,320,256]{3,2,1,0:T(8,128)(2,1)S(1)} collective-permute-done((bf16[2,2,320,256]{3,2,1,0:T(8,128)(2,1)S(1)}, bf16[2,2,320,256]{3,2,1,0:T(8,128)(2,1)S(1)}, u32[]{:S(2)}, u32[]{:S(2)}) %collective-permute-start.3) | collective-permute-done | bytes 655392 | tf_op jit(solution)/shard_map/ppermute | solution.py:259
  54.4 5.4 %collective-permute-start.6 = (bf16[3,336,128]{2,1,0:T(8,128)(2,1)S(1)}, bf16[3,336,128]{2,1,0:T(8,128)(2,1)S(1)}, u32[]{:S(2)}, u32[]{:S(2)}) collective-permute-start(bf16[3,336,128]{2,1,0:T(8,128)(2,1)S(1)} %pad_add_fusion.7), channel_id=1, source_target_pairs={{0,8},{2,10},{4,12},{6,14},{8,0},{10,2},{12,4},{14,6},{16,24},{18,... | collective-permute-start | bytes 774152 | tf_op jit(solution)/shard_map/ppermute | solution.py:259
  62.8 10.2 %attend_slots.4 = (f32[4,2,1,320]{3,2,1,0:T(1,128)S(1)}, f32[4,2,1,320]{3,2,1,0:T(1,128)S(1)}, f32[4,2,128,320]{3,2,1,0:T(8,128)S(1)}) custom-call(s32[4,8]{1,0:T(4,128)S(1)} %get-tuple-element.133.flags_ref, bf16[3,336,256]{2,1,0:T(8,128)(2,1)S(1)} %get-tuple-element.139.refs_0_, bf16[3,336,256]{2,1,0:T(8,128)(2,1)S(1)} %collective-permute-done.refs_1_, ...), custom_call_target="tpu_custom_call" | custom-call | tf_op jit(solution)/shard_map/attend_slots/pallas_call | solution.py:223
  73.1 7.8 %collective-permute-done.7.refs_2_ = bf16[3,336,128]{2,1,0:T(8,128)(2,1)S(1)} collective-permute-done((bf16[3,336,128]{2,1,0:T(8,128)(2,1)S(1)}, bf16[3,336,128]{2,1,0:T(8,128)(2,1)S(1)}, u32[]{:S(2)}, u32[]{:S(2)}) %collective-permute-start.7) | collective-permute-done | bytes 258080 | tf_op jit(solution)/shard_map/ppermute | solution.py:259
  83.7 17.0 %attend_slots.5 = (bf16[320,256]{1,0:T(8,128)(2,1)S(1)}, bf16[320,256]{1,0:T(8,128)(2,1)S(1)}, bf16[320,256]{1,0:T(8,128)(2,1)S(1)}, bf16[320,256]{1,0:T(8,128)(2,1)S(1)}) custom-call(s32[4,8]{1,0:T(4,128)S(1)} %get-tuple-element.134.flags_ref, bf16[3,336,256]{2,1,0:T(8,128)(2,1)S(1)} %get-tuple-element.139.refs_0_, ...), custom_call_target="tpu_custom_call" | custom-call | tf_op jit(solution)/shard_map/attend_slots/pallas_call | solution.py:223
  100.7 2.5 %collective-permute-start.20 = (bf16[320,256]{1,0:T(8,128)(2,1)S(1)}, bf16[320,256]{1,0:T(8,128)(2,1)S(1)}, u32[]{:S(2)}, u32[]{:S(2)}) collective-permute-start(bf16[320,256]{1,0:T(8,128)(2,1)S(1)} %get-tuple-element.77), channel_id=1, source_target_pairs={{0,24},{2,26},{4,28},{6,30},{8,16},{10,18},{12,20},{14,22},{16,8},... | collective-permute-start | bytes 491528 | tf_op jit(solution)/shard_map/ppermute | solution.py:259
  103.3 4.0 %collective-permute-start.19 = (bf16[320,256]{1,0:T(8,128)(2,1)S(1)}, bf16[320,256]{1,0:T(8,128)(2,1)S(1)}, u32[]{:S(2)}, u32[]{:S(2)}) collective-permute-start(bf16[320,256]{1,0:T(8,128)(2,1)S(1)} %get-tuple-element.76), channel_id=1, source_target_pairs={{0,16},{2,18},{4,20},{6,22},{8,24},{10,26},{12,28},{14,30},{16,0},... | collective-permute-start | bytes 491528 | tf_op jit(solution)/shard_map/ppermute | solution.py:259
  108.0 7.5 %attend_slots.6 = (f32[4,1,1,320]{3,2,1,0:T(1,128)S(1)}, f32[4,1,1,320]{3,2,1,0:T(1,128)S(1)}, f32[4,1,128,320]{3,2,1,0:T(8,128)S(1)}) custom-call(s32[4,8]{1,0:T(4,128)S(1)} %get-tuple-element.133.flags_ref, bf16[3,336,128]{2,1,0:T(8,128)(2,1)S(1)} %get-tuple-element.78.refs_0_, bf16[3,336,128]{2,1,0:T(8,128)(2,1)S(1)} %collective-permute-done.6.refs_1_, ...), custom_call_target="tpu_custom_call" | custom-call | tf_op jit(solution)/shard_map/attend_slots/pallas_call | solution.py:223
  115.6 2.9 %collective-permute-done.19 = bf16[320,256]{1,0:T(8,128)(2,1)S(1)} collective-permute-done((bf16[320,256]{1,0:T(8,128)(2,1)S(1)}, bf16[320,256]{1,0:T(8,128)(2,1)S(1)}, u32[]{:S(2)}, u32[]{:S(2)}) %collective-permute-start.19) | collective-permute-done | bytes 163872 | tf_op jit(solution)/shard_map/ppermute | solution.py:259
  118.6 2.1 %convolution_convert_fusion = bf16[320,1536]{1,0:T(8,128)(2,1)} fusion(bf16[320,1024]{1,0:T(8,128)(2,1)S(1)} %pad_maximum_fusion.6, bf16[1024,1536]{1,0:T(8,128)(2,1)S(1)} %pad_maximum_fusion.1), kind=kOutput, calls=%fused_computation.5 | convolution fusion | flops 1007124480 | bytes 4784128 | tf_op jit(solution)/shard_map/dot_general | solution.py:350
  122.2 10.9 %attend_slots.7 = (bf16[320,128]{1,0:T(8,128)(2,1)S(1)}, bf16[320,128]{1,0:T(8,128)(2,1)S(1)}, bf16[320,128]{1,0:T(8,128)(2,1)S(1)}, bf16[320,128]{1,0:T(8,128)(2,1)S(1)}) custom-call(s32[4,8]{1,0:T(4,128)S(1)} %get-tuple-element.134.flags_ref, bf16[3,336,128]{2,1,0:T(8,128)(2,1)S(1)} %get-tuple-element.78.refs_0_, ...), custom_call_target="tpu_custom_call" | custom-call | tf_op jit(solution)/shard_map/attend_slots/pallas_call | solution.py:223
  133.2 3.0 %collective-permute-start.24 = (bf16[320,128]{1,0:T(8,128)(2,1)S(1)}, bf16[320,128]{1,0:T(8,128)(2,1)S(1)}, u32[]{:S(2)}, u32[]{:S(2)}) collective-permute-start(bf16[320,128]{1,0:T(8,128)(2,1)S(1)} %get-tuple-element.90), channel_id=1, source_target_pairs={{0,16},{2,18},{4,20},{6,22},{8,24},{10,26},{12,28},{14,30},{16,0},... | collective-permute-start | bytes 245768 | tf_op jit(solution)/shard_map/ppermute | solution.py:259
  137.6 2.3 %fusion.52 = f32[320,1536]{1,0:T(8,128)S(1)} fusion(bf16[320,1024]{1,0:T(8,128)(2,1)} %copy-done.5, bf16[1024,1536]{1,0:T(8,128)(2,1)S(1)} %copy-done), kind=kOutput, calls=%fused_computation.136 | convolution fusion | flops 1006632960 | bytes 5767168 | tf_op jit(solution)/shard_map/dot_general | solution.py:350
  144.0 1.9 %fusion = f32[320,1536]{1,0:T(8,128)S(1)} fusion(f32[320,1536]{1,0:T(8,128)S(1)} %fusion.52, bf16[320,512]{1,0:T(8,128)(2,1)S(1)} %constant_dynamic-update-slice_fusion, bf16[320,1536]{1,0:T(8,128)(2,1)} %collective-permute-done.27, bf16[128,1536]{1,0:T(8,128)(2,1)S(1)} %copy-done.7, bf16[128,1536]{1,0:T(8,128)(2,1)S(1)} %copy-done.8, ...), kind=kOutput, calls=%fused_computation.4 | convolution fusion | flops 511082496 | bytes 6815744 | tf_op jit(solution)/shard_map/dot_general | solution.py:350
  145.9 4.8 %collective-permute-done.26 = bf16[320,512]{1,0:T(8,128)(2,1)S(1)} collective-permute-done((bf16[320,512]{1,0:T(8,128)(2,1)S(1)}, bf16[320,512]{1,0:T(8,128)(2,1)S(1)}, u32[]{:S(2)}, u32[]{:S(2)}) %collective-permute-start.26) | collective-permute-done | bytes 327712 | tf_op jit(solution)/shard_map/ppermute | solution.py:265
  (114 shorter events, 31.7 us)
Async XLA Ops:
  3.6 23.6 %collective-permute-start = (bf16[3,336,256]{2,1,0:T(8,128)(2,1)}, bf16[3,336,256]{2,1,0:T(8,128)(2,1)S(1)}, u32[]{:S(2)}, u32[]{:S(2)}) collective-permute-start(bf16[3,336,256]{2,1,0:T(8,128)(2,1)} %pad_add_fusion.3), channel_id=1, source_target_pairs={{0,8},{2,10},{4,12},{6,14},{8,0},{10,2},{12,4},{14,6},{16,24},{18,... | collective-permute-start | bytes 1548296 | tf_op jit(solution)/shard_map/ppermute | solution.py:259
  9.0 37.9 %collective-permute-start.1 = (bf16[3,336,256]{2,1,0:T(8,128)(2,1)}, bf16[3,336,256]{2,1,0:T(8,128)(2,1)S(1)}, u32[]{:S(2)}, u32[]{:S(2)}) collective-permute-start(bf16[3,336,256]{2,1,0:T(8,128)(2,1)} %get-tuple-element.140), channel_id=1, source_target_pairs={{0,16},{2,18},{4,20},{6,22},{8,24},{10,26},{12,28},{14,30},{16,0},... | collective-permute-start | bytes 1548296 | tf_op jit(solution)/shard_map/ppermute | solution.py:259
  11.6 35.3 %collective-permute-start.2 = (bf16[3,336,256]{2,1,0:T(8,128)(2,1)}, bf16[3,336,256]{2,1,0:T(8,128)(2,1)S(1)}, u32[]{:S(2)}, u32[]{:S(2)}) collective-permute-start(bf16[3,336,256]{2,1,0:T(8,128)(2,1)} %get-tuple-element.138), channel_id=1, source_target_pairs={{0,24},{2,26},{4,28},{6,30},{8,16},{10,18},{12,20},{14,22},{16,8},... | collective-permute-start | bytes 1548296 | tf_op jit(solution)/shard_map/ppermute | solution.py:259
  15.4 19.0 %collective-permute-start.4 = (bf16[256,1536]{1,0:T(8,128)(2,1)}, bf16[256,1536]{1,0:T(8,128)(2,1)}, u32[]{:S(2)}, u32[]{:S(2)}) collective-permute-start(bf16[256,1536]{1,0:T(8,128)(2,1)} %pad_maximum_fusion.3), channel_id=1, source_target_pairs={{0,1},{1,0},{2,3},{3,2},{4,5},{5,4},{6,7},{7,6},{8,9},{9,8},{10,11... | collective-permute-start | bytes 2359304 | tf_op jit(solution)/shard_map/ppermute | solution.py:265
  34.4 17.3 %collective-permute-start.5 = (bf16[256,1536]{1,0:T(8,128)(2,1)}, bf16[256,1536]{1,0:T(8,128)(2,1)S(1)}, u32[]{:S(2)}, u32[]{:S(2)}) collective-permute-start(bf16[256,1536]{1,0:T(8,128)(2,1)} %collective-permute-done.4), channel_id=1, source_target_pairs={{0,2},{2,0},{4,6},{6,4},{8,10},{10,8},{12,14},{14,12},{16,18},{18,... | collective-permute-start | bytes 2359304 | tf_op jit(solution)/shard_map/ppermute | solution.py:259
  34.5 17.2 %collective-permute-start.3 = (bf16[2,2,320,256]{3,2,1,0:T(8,128)(2,1)S(1)}, bf16[2,2,320,256]{3,2,1,0:T(8,128)(2,1)S(1)}, u32[]{:S(2)}, u32[]{:S(2)}) collective-permute-start(bf16[2,2,320,256]{3,2,1,0:T(8,128)(2,1)S(1)} %pad_maximum_fusion.4.refs_4_), channel_id=1, source_target_pairs={{0,4},{2,6},{4,0},{6,2},{8,12},{10,14},{12,8},{14,10},{16,20},{18,... | collective-permute-start | bytes 1966088 | tf_op jit(solution)/shard_map/ppermute | solution.py:259
  36.2 24.9 %collective-permute-start.9 = (bf16[2,2,320,256]{3,2,1,0:T(8,128)(2,1)S(1)}, bf16[2,2,320,256]{3,2,1,0:T(8,128)(2,1)S(1)}, u32[]{:S(2)}, u32[]{:S(2)}) collective-permute-start(bf16[2,2,320,256]{3,2,1,0:T(8,128)(2,1)S(1)} %pad_maximum_fusion.4.refs_4_), channel_id=1, source_target_pairs={{0,2},{2,0},{4,6},{6,4},{8,10},{10,8},{12,14},{14,12},{16,18},{18,... | collective-permute-start | bytes 1966088 | tf_op jit(solution)/shard_map/ppermute | solution.py:259
  52.7 10.1 %collective-permute-start.10 = (bf16[2,2,320,256]{3,2,1,0:T(8,128)(2,1)S(1)}, bf16[2,2,320,256]{3,2,1,0:T(8,128)(2,1)S(1)}, u32[]{:S(2)}, u32[]{:S(2)}) collective-permute-start(bf16[2,2,320,256]{3,2,1,0:T(8,128)(2,1)S(1)} %pad_maximum_fusion.5.refs_5_), channel_id=1, source_target_pairs={{0,2},{2,0},{4,6},{6,4},{8,10},{10,8},{12,14},{14,12},{16,18},{18,... | collective-permute-start | bytes 1966088 | tf_op jit(solution)/shard_map/ppermute | solution.py:259
  52.8 28.7 %collective-permute-start.11 = (bf16[2,2,320,256]{3,2,1,0:T(8,128)(2,1)S(1)}, bf16[2,2,320,256]{3,2,1,0:T(8,128)(2,1)S(1)}, u32[]{:S(2)}, u32[]{:S(2)}) collective-permute-start(bf16[2,2,320,256]{3,2,1,0:T(8,128)(2,1)S(1)} %pad_maximum_fusion.5.refs_5_), channel_id=1, source_target_pairs={{0,4},{2,6},{4,0},{6,2},{8,12},{10,14},{12,8},{14,10},{16,20},{18,... | collective-permute-start | bytes 1966088 | tf_op jit(solution)/shard_map/ppermute | solution.py:259
  54.4 18.7 %collective-permute-start.6 = (bf16[3,336,128]{2,1,0:T(8,128)(2,1)S(1)}, bf16[3,336,128]{2,1,0:T(8,128)(2,1)S(1)}, u32[]{:S(2)}, u32[]{:S(2)}) collective-permute-start(bf16[3,336,128]{2,1,0:T(8,128)(2,1)S(1)} %pad_add_fusion.7), channel_id=1, source_target_pairs={{0,8},{2,10},{4,12},{6,14},{8,0},{10,2},{12,4},{14,6},{16,24},{18,... | collective-permute-start | bytes 774152 | tf_op jit(solution)/shard_map/ppermute | solution.py:259
  59.8 21.1 %collective-permute-start.7 = (bf16[3,336,128]{2,1,0:T(8,128)(2,1)S(1)}, bf16[3,336,128]{2,1,0:T(8,128)(2,1)S(1)}, u32[]{:S(2)}, u32[]{:S(2)}) collective-permute-start(bf16[3,336,128]{2,1,0:T(8,128)(2,1)S(1)} %get-tuple-element.63), channel_id=1, source_target_pairs={{0,16},{2,18},{4,20},{6,22},{8,24},{10,26},{12,28},{14,30},{16,0},... | collective-permute-start | bytes 774152 | tf_op jit(solution)/shard_map/ppermute | solution.py:259
  61.1 19.8 %collective-permute-start.8 = (bf16[3,336,128]{2,1,0:T(8,128)(2,1)S(1)}, bf16[3,336,128]{2,1,0:T(8,128)(2,1)S(1)}, u32[]{:S(2)}, u32[]{:S(2)}) collective-permute-start(bf16[3,336,128]{2,1,0:T(8,128)(2,1)S(1)} %get-tuple-element.64), channel_id=1, source_target_pairs={{0,24},{2,26},{4,28},{6,30},{8,16},{10,18},{12,20},{14,22},{16,8},... | collective-permute-start | bytes 774152 | tf_op jit(solution)/shard_map/ppermute | solution.py:259
  62.8 20.6 %collective-permute-start.12 = (bf16[2,2,320,256]{3,2,1,0:T(8,128)(2,1)S(1)}, bf16[2,2,320,256]{3,2,1,0:T(8,128)(2,1)S(1)}, u32[]{:S(2)}, u32[]{:S(2)}) collective-permute-start(bf16[2,2,320,256]{3,2,1,0:T(8,128)(2,1)S(1)} %collective-permute-done.3.refs_4_), channel_id=1, source_target_pairs={{0,2},{2,0},{4,6},{6,4},{8,10},{10,8},{12,14},{14,12},{16,18},{18,... | collective-permute-start | bytes 1966088 | tf_op jit(solution)/shard_map/ppermute | solution.py:259
  80.9 22.4 %collective-permute-start.14 = (bf16[2,2,320,128]{3,2,1,0:T(8,128)(2,1)S(1)}, bf16[2,2,320,128]{3,2,1,0:T(8,128)(2,1)S(1)}, u32[]{:S(2)}, u32[]{:S(2)}) collective-permute-start(bf16[2,2,320,128]{3,2,1,0:T(8,128)(2,1)S(1)} %pad_maximum_fusion.7.refs_4_), channel_id=1, source_target_pairs={{0,4},{2,6},{4,0},{6,2},{8,12},{10,14},{12,8},{14,10},{16,20},{18,... | collective-permute-start | bytes 983048 | tf_op jit(solution)/shard_map/ppermute | solution.py:259
  81.6 25.7 %collective-permute-start.15 = (bf16[2,2,320,128]{3,2,1,0:T(8,128)(2,1)S(1)}, bf16[2,2,320,128]{3,2,1,0:T(8,128)(2,1)}, u32[]{:S(2)}, u32[]{:S(2)}) collective-permute-start(bf16[2,2,320,128]{3,2,1,0:T(8,128)(2,1)S(1)} %pad_maximum_fusion.8.refs_5_), channel_id=1, source_target_pairs={{0,4},{2,6},{4,0},{6,2},{8,12},{10,14},{12,8},{14,10},{16,20},{18,... | collective-permute-start | bytes 983048 | tf_op jit(solution)/shard_map/ppermute | solution.py:259
  83.2 24.3 %collective-permute-start.21 = (bf16[2,2,320,128]{3,2,1,0:T(8,128)(2,1)S(1)}, bf16[2,2,320,128]{3,2,1,0:T(8,128)(2,1)S(1)}, u32[]{:S(2)}, u32[]{:S(2)}) collective-permute-start(bf16[2,2,320,128]{3,2,1,0:T(8,128)(2,1)S(1)} %pad_maximum_fusion.7.refs_4_), channel_id=1, source_target_pairs={{0,2},{2,0},{4,6},{6,4},{8,10},{10,8},{12,14},{14,12},{16,18},{18,... | collective-permute-start | bytes 983048 | tf_op jit(solution)/shard_map/ppermute | solution.py:259
  83.4 24.1 %collective-permute-start.22 = (bf16[2,2,320,128]{3,2,1,0:T(8,128)(2,1)S(1)}, bf16[2,2,320,128]{3,2,1,0:T(8,128)(2,1)S(1)}, u32[]{:S(2)}, u32[]{:S(2)}) collective-permute-start(bf16[2,2,320,128]{3,2,1,0:T(8,128)(2,1)S(1)} %pad_maximum_fusion.8.refs_5_), channel_id=1, source_target_pairs={{0,2},{2,0},{4,6},{6,4},{8,10},{10,8},{12,14},{14,12},{16,18},{18,... | collective-permute-start | bytes 983048 | tf_op jit(solution)/shard_map/ppermute | solution.py:259
  100.7 14.8 %collective-permute-start.20 = (bf16[320,256]{1,0:T(8,128)(2,1)S(1)}, bf16[320,256]{1,0:T(8,128)(2,1)S(1)}, u32[]{:S(2)}, u32[]{:S(2)}) collective-permute-start(bf16[320,256]{1,0:T(8,128)(2,1)S(1)} %get-tuple-element.77), channel_id=1, source_target_pairs={{0,24},{2,26},{4,28},{6,30},{8,16},{10,18},{12,20},{14,22},{16,8},... | collective-permute-start | bytes 491528 | tf_op jit(solution)/shard_map/ppermute | solution.py:259
  103.3 15.2 %collective-permute-start.19 = (bf16[320,256]{1,0:T(8,128)(2,1)S(1)}, bf16[320,256]{1,0:T(8,128)(2,1)S(1)}, u32[]{:S(2)}, u32[]{:S(2)}) collective-permute-start(bf16[320,256]{1,0:T(8,128)(2,1)S(1)} %get-tuple-element.76), channel_id=1, source_target_pairs={{0,16},{2,18},{4,20},{6,22},{8,24},{10,26},{12,28},{14,30},{16,0},... | collective-permute-start | bytes 491528 | tf_op jit(solution)/shard_map/ppermute | solution.py:259
  107.3 11.1 %collective-permute-start.18 = (bf16[320,256]{1,0:T(8,128)(2,1)S(1)}, bf16[320,256]{1,0:T(8,128)(2,1)S(1)}, u32[]{:S(2)}, u32[]{:S(2)}) collective-permute-start(bf16[320,256]{1,0:T(8,128)(2,1)S(1)} %get-tuple-element.75), channel_id=1, source_target_pairs={{0,8},{2,10},{4,12},{6,14},{8,0},{10,2},{12,4},{14,6},{16,24},{18,... | collective-permute-start | bytes 491528 | tf_op jit(solution)/shard_map/ppermute | solution.py:259
  107.5 14.7 %collective-permute-start.16 = (bf16[2,2,320,128]{3,2,1,0:T(8,128)(2,1)S(1)}, bf16[2,2,320,128]{3,2,1,0:T(8,128)(2,1)S(1)}, u32[]{:S(2)}, u32[]{:S(2)}) collective-permute-start(bf16[2,2,320,128]{3,2,1,0:T(8,128)(2,1)S(1)} %collective-permute-done.14.refs_4_), channel_id=1, source_target_pairs={{0,2},{2,0},{4,6},{6,4},{8,10},{10,8},{12,14},{14,12},{16,18},{18,... | collective-permute-start | bytes 983048 | tf_op jit(solution)/shard_map/ppermute | solution.py:259
  107.5 14.7 %collective-permute-start.17 = (bf16[2,2,320,128]{3,2,1,0:T(8,128)(2,1)}, bf16[2,2,320,128]{3,2,1,0:T(8,128)(2,1)S(1)}, u32[]{:S(2)}, u32[]{:S(2)}) collective-permute-start(bf16[2,2,320,128]{3,2,1,0:T(8,128)(2,1)} %collective-permute-done.15.refs_5_), channel_id=1, source_target_pairs={{0,2},{2,0},{4,6},{6,4},{8,10},{10,8},{12,14},{14,12},{16,18},{18,... | collective-permute-start | bytes 983048 | tf_op jit(solution)/shard_map/ppermute | solution.py:259
  120.7 23.3 %collective-permute-start.27 = (bf16[320,1536]{1,0:T(8,128)(2,1)}, bf16[320,1536]{1,0:T(8,128)(2,1)}, u32[]{:S(2)}, u32[]{:S(2)}) collective-permute-start(bf16[320,1536]{1,0:T(8,128)(2,1)} %convolution_convert_fusion), channel_id=1, source_target_pairs={{0,1},{1,0},{2,3},{3,2},{4,5},{5,4},{6,7},{7,6},{8,9},{9,8},{10,11... | collective-permute-start | bytes 2949128 | tf_op jit(solution)/shard_map/ppermute | solution.py:265
  142.7 8.1 %collective-permute-start.26 = (bf16[320,512]{1,0:T(8,128)(2,1)S(1)}, bf16[320,512]{1,0:T(8,128)(2,1)S(1)}, u32[]{:S(2)}, u32[]{:S(2)}) collective-permute-start(bf16[320,512]{1,0:T(8,128)(2,1)S(1)} %constant_dynamic-update-slice_fusion), channel_id=1, source_target_pairs={{0,1},{1,0},{2,3},{3,2},{4,5},{5,4},{6,7},{7,6},{8,9},{9,8},{10,11... | collective-permute-start | bytes 983048 | tf_op jit(solution)/shard_map/ppermute | solution.py:265
  (15 other events, 98.4 us)

commit v4 on v3

--- a/solution.py
+++ b/solution.py
@@ -313,19 +313,19 @@
     part = across(
         jnp.concatenate(weight_rows(weight, 1 - side, (2 * core, 2 * core + 1), final))
     )
-    rest = swap(part, 1)
+    far_rows = jnp.concatenate([part, swap(part, 1)])
     for c in range(1, len(chunks)):
         arrays = after(arrays, packed[-1])
         packed.append(pack_heads(arrays, starts[c], chunks[c]))
 
-    def receive(pieces, *gate):
+    def receive(pieces, gate=None):
         pieces = [pieces[0]] + [swap_planes(pieces[k], k) for k in range(1, PLANES)]
-        if gate:
-            pieces[1:] = after(pieces[1:], *gate)
+        if gate is not None:
+            pieces[1:] = after(pieces[1:], gate)
         low = stack(pieces[:2])
         chip_low = swap(low, 2)
-        if not gate:
-            pieces[2:] = after(pieces[2:], chip_low, weight_sides, rest)
+        if gate is None:
+            pieces[2:] = after(pieces[2:], chip_low, weight_sides, far_rows)
         high = stack(pieces[2:])
         chip_high = swap(high, 2)
         mine = [low, high, swap(low, 1), swap(high, 1)]
@@ -380,9 +380,12 @@
         mixed = mixed + taken.astype(F32)
     far, mixed = lax.optimization_barrier((far, mixed))
     pair_width = far.shape[1] // 2
-    for at, held_rows in ((core, part), (1 - core, rest)):
-        columns = lax.dynamic_slice_in_dim(far, at * pair_width, pair_width, 1)
-        mixed = mixed + jnp.dot(columns, held_rows, preferred_element_type=F32)
+    pairs = [
+        lax.dynamic_slice_in_dim(far, at * pair_width, pair_width, 1) for at in (core, 1 - core)
+    ]
+    mixed = mixed + jnp.dot(
+        jnp.concatenate(pairs, axis=1), far_rows, preferred_element_type=F32
+    )
     return mixed.astype(BF16)
 
 

time: 154 us -> 151 us (0.981)
  Pallas kernels: 45.7 us -> 43.7 us
  starting transfers between devices: 35.4 us -> 37.1 us
    ppermute x25, waiting for transfers between devices: 29.3 us -> 25.8 us  [swap(): return lax.ppermute(value, 'seq', [(i, i ^ bits) for i in range(blocks)])]
    ppermute x3, waiting for transfers between devices: 12.7 us -> 15.1 us  [across(): return lax.ppermute(value, 'head', [(0, 1), (1, 0)])]
    pallas_call x4, Pallas kernels: 45.7 us -> 43.7 us  [attend(): pl.pallas_call(functools.partial(attend_kernel, heads, plan, not state, l...]
    ppermute x25, starting transfers between devices: 31.6 us -> 33.3 us  [swap(): return lax.ppermute(value, 'seq', [(i, i ^ bits) for i in range(blocks)])]
  transfers between devices with their start and end apart: 28 -> 28, of which waited for: 10 -> 9; matrix products, arithmetic and copies ran while one was open for 15% -> 16% of each run, Pallas kernels for 30% -> 29%
where the time goes in v4:
time: 151 us
  Pallas kernels  43.7 us (29%)
  waiting for transfers between devices  40.9 us (27%)
  starting transfers between devices  37.1 us (25%)
  local copies, waits for them, and re-layouts  14.7 us (10%)
  matrix products  8.02 us (5%)
  other arithmetic  6.6 us (4%)
    pallas_call x4, Pallas kernels, attend(): pl.pallas_call(functools.partial(attend_kernel, heads, plan, not state, l...  43.7 us
    ppermute x25, starting transfers between devices, swap(): return lax.ppermute(value, 'seq', [(i, i ^ bits) for i in range(blocks)])  33.3 us
    ppermute x25, waiting for transfers between devices, swap(): return lax.ppermute(value, 'seq', [(i, i ^ bits) for i in range(blocks)])  25.8 us
    ppermute x3, waiting for transfers between devices, across(): return lax.ppermute(value, 'head', [(0, 1), (1, 0)])  15.1 us
    another operation x11, local copies, waits for them, and re-layouts, pack_heads(): jnp.stack([lax.dynamic_slice_in_dim(array, first, heads * HD, 1) for arra...  7 us
    dot_general x3, matrix products, project(): jnp.dot(near, weight_sides[at][c], preferred_element_type=F32)  6.39 us
    dynamic_slice x2, local copies, waits for them, and re-layouts, weight_rows(): lax.dynamic_slice(weight, (((plane ^ k) * per_plane + starts[c]) * HD, si...  6.08 us
    ppermute x3, starting transfers between devices, across(): return lax.ppermute(value, 'head', [(0, 1), (1, 0)])  3.79 us
  transfers between devices with their start and end apart: 28, of which 9 were waited for; matrix products, arithmetic and copies ran while one was open for 16% of the time, Pallas kernels for 29%

profile of v4, /device:TPU:0, one launch (start us, length us, event | category | flops | bytes accessed | tf_op | source)
XLA Modules:
  0.0 151.4 jit_solution(10253679934950604831)
XLA Ops:
  3.6 3.0 %collective-permute-start = (bf16[3,336,256]{2,1,0:T(8,128)(2,1)}, bf16[3,336,256]{2,1,0:T(8,128)(2,1)S(1)}, u32[]{:S(2)}, u32[]{:S(2)}) collective-permute-start(bf16[3,336,256]{2,1,0:T(8,128)(2,1)} %pad_add_fusion.3), channel_id=1, source_target_pairs={{0,8},{2,10},{4,12},{6,14},{8,0},{10,2},{12,4},{14,6},{16,24},{18,... | collective-permute-start | bytes 1548296 | tf_op jit(solution)/shard_map/ppermute | solution.py:259
  9.0 2.6 %collective-permute-start.1 = (bf16[3,336,256]{2,1,0:T(8,128)(2,1)}, bf16[3,336,256]{2,1,0:T(8,128)(2,1)S(1)}, u32[]{:S(2)}, u32[]{:S(2)}) collective-permute-start(bf16[3,336,256]{2,1,0:T(8,128)(2,1)} %get-tuple-element.141), channel_id=1, source_target_pairs={{0,16},{2,18},{4,20},{6,22},{8,24},{10,26},{12,28},{14,30},{16,0},... | collective-permute-start | bytes 1548296 | tf_op jit(solution)/shard_map/ppermute | solution.py:259
  11.6 2.9 %fusion.48 = (bf16[128,1536]{1,0:T(8,128)(2,1)}, bf16[128,1536]{1,0:T(8,128)(2,1)S(1)}, bf16[128,1536]{1,0:T(8,128)(2,1)S(1)}, bf16[128,1536]{1,0:T(8,128)(2,1)}...) fusion(bf16[1536,3072]{1,0:T(8,128)(2,1)} %param.11, s32[]{:T(128)S(6)} %select_n.56, s32[]{:T(128)S(6)} %select_n.55, ...), kind=kLoop, calls=%fused_computation.136 | loop fusion | bytes 4718624 | tf_op jit(solution)/shard_map/dynamic_slice | solution.py:296
  17.1 3.2 %fusion.49 = (bf16[256,1536]{1,0:T(8,128)(2,1)S(1)}, bf16[256,1536]{1,0:T(8,128)(2,1)S(1)}, bf16[256,1536]{1,0:T(8,128)(2,1)S(1)}, bf16[256,1536]{1,0:T(8,128)(2...) fusion(bf16[1536,3072]{1,0:T(8,128)(2,1)} %param.11, ...), kind=kLoop, calls=%fused_computation.137 | loop fusion | bytes 12582936 | tf_op jit(solution)/shard_map/dynamic_slice | solution.py:296
  24.5 1.8 %pad_maximum_fusion = bf16[1024,1536]{1,0:T(8,128)(2,1)} fusion(bf16[256,1536]{1,0:T(8,128)(2,1)S(1)} %get-tuple-element.111, bf16[256,1536]{1,0:T(8,128)(2,1)S(1)} %get-tuple-element.112, bf16[256,1536]{1,0:T(8,128)(2,1)S(1)} %get-tuple-element.113, bf16[256,1536]{1,0:T(8,128)(2,1)S(1)} %get-tuple-element.114), kind=kLoop, calls=%fused_computation | loop fusion | flops 12582912 | bytes 6291456 | tf_op jit(solution)/shard_map/concatenate | solution.py:307
  26.6 7.8 %collective-permute-done.4 = bf16[256,1536]{1,0:T(8,128)(2,1)} collective-permute-done((bf16[256,1536]{1,0:T(8,128)(2,1)}, bf16[256,1536]{1,0:T(8,128)(2,1)}, u32[]{:S(2)}, u32[]{:S(2)}) %collective-permute-start.4) | collective-permute-done | bytes 786464 | tf_op jit(solution)/shard_map/ppermute | solution.py:265
  37.6 9.3 %collective-permute-done.1.refs_2_ = bf16[3,336,256]{2,1,0:T(8,128)(2,1)S(1)} collective-permute-done((bf16[3,336,256]{2,1,0:T(8,128)(2,1)}, bf16[3,336,256]{2,1,0:T(8,128)(2,1)S(1)}, u32[]{:S(2)}, u32[]{:S(2)}) %collective-permute-start.1) | collective-permute-done | bytes 516128 | tf_op jit(solution)/shard_map/ppermute | solution.py:259
  46.9 4.8 %collective-permute-done.3.refs_4_ = bf16[2,2,320,256]{3,2,1,0:T(8,128)(2,1)S(1)} collective-permute-done((bf16[2,2,320,256]{3,2,1,0:T(8,128)(2,1)S(1)}, bf16[2,2,320,256]{3,2,1,0:T(8,128)(2,1)S(1)}, u32[]{:S(2)}, u32[]{:S(2)}) %collective-permute-start.3) | collective-permute-done | bytes 655392 | tf_op jit(solution)/shard_map/ppermute | solution.py:259
  53.5 5.4 %collective-permute-start.6 = (bf16[3,336,128]{2,1,0:T(8,128)(2,1)S(1)}, bf16[3,336,128]{2,1,0:T(8,128)(2,1)S(1)}, u32[]{:S(2)}, u32[]{:S(2)}) collective-permute-start(bf16[3,336,128]{2,1,0:T(8,128)(2,1)S(1)} %pad_add_fusion.7), channel_id=1, source_target_pairs={{0,8},{2,10},{4,12},{6,14},{8,0},{10,2},{12,4},{14,6},{16,24},{18,... | collective-permute-start | bytes 774152 | tf_op jit(solution)/shard_map/ppermute | solution.py:259
  61.9 11.5 %attend_slots.4 = (f32[4,2,1,320]{3,2,1,0:T(1,128)S(1)}, f32[4,2,1,320]{3,2,1,0:T(1,128)S(1)}, f32[4,2,128,320]{3,2,1,0:T(8,128)S(1)}) custom-call(s32[4,8]{1,0:T(4,128)S(1)} %get-tuple-element.135.flags_ref, bf16[3,336,256]{2,1,0:T(8,128)(2,1)S(1)} %get-tuple-element.140.refs_0_, bf16[3,336,256]{2,1,0:T(8,128)(2,1)S(1)} %collective-permute-done.refs_1_, ...), custom_call_target="tpu_custom_call" | custom-call | tf_op jit(solution)/shard_map/attend_slots/pallas_call | solution.py:223
  73.4 6.5 %collective-permute-done.7.refs_2_ = bf16[3,336,128]{2,1,0:T(8,128)(2,1)S(1)} collective-permute-done((bf16[3,336,128]{2,1,0:T(8,128)(2,1)S(1)}, bf16[3,336,128]{2,1,0:T(8,128)(2,1)S(1)}, u32[]{:S(2)}, u32[]{:S(2)}) %collective-permute-start.7) | collective-permute-done | bytes 258080 | tf_op jit(solution)/shard_map/ppermute | solution.py:259
  82.8 14.5 %attend_slots.5 = (bf16[320,256]{1,0:T(8,128)(2,1)S(1)}, bf16[320,256]{1,0:T(8,128)(2,1)S(1)}, bf16[320,256]{1,0:T(8,128)(2,1)S(1)}, bf16[320,256]{1,0:T(8,128)(2,1)S(1)}) custom-call(s32[4,8]{1,0:T(4,128)S(1)} %get-tuple-element.136.flags_ref, bf16[3,336,256]{2,1,0:T(8,128)(2,1)S(1)} %get-tuple-element.140.refs_0_, ...), custom_call_target="tpu_custom_call" | custom-call | tf_op jit(solution)/shard_map/attend_slots/pallas_call | solution.py:223
  97.2 2.5 %collective-permute-start.20 = (bf16[320,256]{1,0:T(8,128)(2,1)S(1)}, bf16[320,256]{1,0:T(8,128)(2,1)S(1)}, u32[]{:S(2)}, u32[]{:S(2)}) collective-permute-start(bf16[320,256]{1,0:T(8,128)(2,1)S(1)} %get-tuple-element.77), channel_id=1, source_target_pairs={{0,24},{2,26},{4,28},{6,30},{8,16},{10,18},{12,20},{14,22},{16,8},... | collective-permute-start | bytes 491528 | tf_op jit(solution)/shard_map/ppermute | solution.py:259
  99.8 4.0 %collective-permute-start.19 = (bf16[320,256]{1,0:T(8,128)(2,1)S(1)}, bf16[320,256]{1,0:T(8,128)(2,1)S(1)}, u32[]{:S(2)}, u32[]{:S(2)}) collective-permute-start(bf16[320,256]{1,0:T(8,128)(2,1)S(1)} %get-tuple-element.76), channel_id=1, source_target_pairs={{0,16},{2,18},{4,20},{6,22},{8,24},{10,26},{12,28},{14,30},{16,0},... | collective-permute-start | bytes 491528 | tf_op jit(solution)/shard_map/ppermute | solution.py:259
  104.0 2.2 %collective-permute-start.16 = (bf16[2,2,320,128]{3,2,1,0:T(8,128)(2,1)S(1)}, bf16[2,2,320,128]{3,2,1,0:T(8,128)(2,1)S(1)}, u32[]{:S(2)}, u32[]{:S(2)}) collective-permute-start(bf16[2,2,320,128]{3,2,1,0:T(8,128)(2,1)S(1)} %collective-permute-done.14.refs_4_), channel_id=1, source_target_pairs={{0,2},{2,0},{4,6},{6,4},{8,10},{10,8},{12,14},{14,12},{16,18},{18,... | collective-permute-start | bytes 983048 | tf_op jit(solution)/shard_map/ppermute | solution.py:259
  106.3 8.3 %attend_slots.6 = (f32[4,1,1,320]{3,2,1,0:T(1,128)S(1)}, f32[4,1,1,320]{3,2,1,0:T(1,128)S(1)}, f32[4,1,128,320]{3,2,1,0:T(8,128)S(1)}) custom-call(s32[4,8]{1,0:T(4,128)S(1)} %get-tuple-element.135.flags_ref, bf16[3,336,128]{2,1,0:T(8,128)(2,1)S(1)} %get-tuple-element.78.refs_0_, bf16[3,336,128]{2,1,0:T(8,128)(2,1)S(1)} %collective-permute-done.6.refs_1_, ...), custom_call_target="tpu_custom_call" | custom-call | tf_op jit(solution)/shard_map/attend_slots/pallas_call | solution.py:223
  115.9 2.1 %convolution_convert_fusion = bf16[320,1536]{1,0:T(8,128)(2,1)} fusion(bf16[320,1024]{1,0:T(8,128)(2,1)S(1)} %pad_maximum_fusion.6, bf16[1024,1536]{1,0:T(8,128)(2,1)S(1)} %pad_maximum_fusion.1), kind=kOutput, calls=%fused_computation.6 | convolution fusion | flops 1007124480 | bytes 4784128 | tf_op jit(solution)/shard_map/dot_general | solution.py:350
  119.5 9.4 %attend_slots.7 = (bf16[320,128]{1,0:T(8,128)(2,1)S(1)}, bf16[320,128]{1,0:T(8,128)(2,1)S(1)}, bf16[320,128]{1,0:T(8,128)(2,1)S(1)}, bf16[320,128]{1,0:T(8,128)(2,1)S(1)}) custom-call(s32[4,8]{1,0:T(4,128)S(1)} %get-tuple-element.136.flags_ref, bf16[3,336,128]{2,1,0:T(8,128)(2,1)S(1)} %get-tuple-element.78.refs_0_, ...), custom_call_target="tpu_custom_call" | custom-call | tf_op jit(solution)/shard_map/attend_slots/pallas_call | solution.py:223
  129.4 3.1 %collective-permute-start.24 = (bf16[320,128]{1,0:T(8,128)(2,1)S(1)}, bf16[320,128]{1,0:T(8,128)(2,1)S(1)}, u32[]{:S(2)}, u32[]{:S(2)}) collective-permute-start(bf16[320,128]{1,0:T(8,128)(2,1)S(1)} %get-tuple-element.90), channel_id=1, source_target_pairs={{0,16},{2,18},{4,20},{6,22},{8,24},{10,26},{12,28},{14,30},{16,0},... | collective-permute-start | bytes 245768 | tf_op jit(solution)/shard_map/ppermute | solution.py:259
  133.5 2.3 %fusion.51 = f32[320,1536]{1,0:T(8,128)S(1)} fusion(bf16[320,1024]{1,0:T(8,128)(2,1)} %copy-done.5, bf16[1024,1536]{1,0:T(8,128)(2,1)S(1)} %copy-done.2), kind=kOutput, calls=%fused_computation.139 | convolution fusion | flops 1006632960 | bytes 5767168 | tf_op jit(solution)/shard_map/dot_general | solution.py:350
  137.1 2.7 %collective-permute-done.25 = bf16[320,128]{1,0:T(8,128)(2,1)S(1)} collective-permute-done((bf16[320,128]{1,0:T(8,128)(2,1)S(1)}, bf16[320,128]{1,0:T(8,128)(2,1)S(1)}, u32[]{:S(2)}, u32[]{:S(2)}) %collective-permute-start.25) | collective-permute-done | bytes 81952 | tf_op jit(solution)/shard_map/ppermute | solution.py:259
  140.4 2.4 %collective-permute-done.27 = bf16[320,1536]{1,0:T(8,128)(2,1)} collective-permute-done((bf16[320,1536]{1,0:T(8,128)(2,1)}, bf16[320,1536]{1,0:T(8,128)(2,1)}, u32[]{:S(2)}, u32[]{:S(2)}) %collective-permute-start.27) | collective-permute-done | bytes 983072 | tf_op jit(solution)/shard_map/ppermute | solution.py:265
  142.9 2.0 %fusion = f32[320,1536]{1,0:T(8,128)S(1)} fusion(f32[320,1536]{1,0:T(8,128)S(1)} %fusion.51, bf16[320,512]{1,0:T(8,128)(2,1)S(1)} %constant_dynamic-update-slice_fusion.2, bf16[320,1536]{1,0:T(8,128)(2,1)} %collective-permute-done.27, bf16[128,1536]{1,0:T(8,128)(2,1)S(1)} %copy-done.7, bf16[128,1536]{1,0:T(8,128)(2,1)S(1)} %copy-done.8, ...), kind=kOutput, calls=%fused_computation.4 | convolution fusion | flops 511082496 | bytes 6815744 | tf_op jit(solution)/shard_map/dot_general | solution.py:350
  144.9 4.9 %collective-permute-done.26 = bf16[320,512]{1,0:T(8,128)(2,1)S(1)} collective-permute-done((bf16[320,512]{1,0:T(8,128)(2,1)S(1)}, bf16[320,512]{1,0:T(8,128)(2,1)S(1)}, u32[]{:S(2)}, u32[]{:S(2)}) %collective-permute-start.26) | collective-permute-done | bytes 327712 | tf_op jit(solution)/shard_map/ppermute | solution.py:265
  (116 shorter events, 31.7 us)
Async XLA Ops:
  3.6 30.8 %collective-permute-start = (bf16[3,336,256]{2,1,0:T(8,128)(2,1)}, bf16[3,336,256]{2,1,0:T(8,128)(2,1)S(1)}, u32[]{:S(2)}, u32[]{:S(2)}) collective-permute-start(bf16[3,336,256]{2,1,0:T(8,128)(2,1)} %pad_add_fusion.3), channel_id=1, source_target_pairs={{0,8},{2,10},{4,12},{6,14},{8,0},{10,2},{12,4},{14,6},{16,24},{18,... | collective-permute-start | bytes 1548296 | tf_op jit(solution)/shard_map/ppermute | solution.py:259
  9.0 37.9 %collective-permute-start.1 = (bf16[3,336,256]{2,1,0:T(8,128)(2,1)}, bf16[3,336,256]{2,1,0:T(8,128)(2,1)S(1)}, u32[]{:S(2)}, u32[]{:S(2)}) collective-permute-start(bf16[3,336,256]{2,1,0:T(8,128)(2,1)} %get-tuple-element.141), channel_id=1, source_target_pairs={{0,16},{2,18},{4,20},{6,22},{8,24},{10,26},{12,28},{14,30},{16,0},... | collective-permute-start | bytes 1548296 | tf_op jit(solution)/shard_map/ppermute | solution.py:259
  11.6 35.3 %collective-permute-start.2 = (bf16[3,336,256]{2,1,0:T(8,128)(2,1)}, bf16[3,336,256]{2,1,0:T(8,128)(2,1)S(1)}, u32[]{:S(2)}, u32[]{:S(2)}) collective-permute-start(bf16[3,336,256]{2,1,0:T(8,128)(2,1)} %get-tuple-element.142), channel_id=1, source_target_pairs={{0,24},{2,26},{4,28},{6,30},{8,16},{10,18},{12,20},{14,22},{16,8},... | collective-permute-start | bytes 1548296 | tf_op jit(solution)/shard_map/ppermute | solution.py:259
  15.4 19.0 %collective-permute-start.4 = (bf16[256,1536]{1,0:T(8,128)(2,1)}, bf16[256,1536]{1,0:T(8,128)(2,1)}, u32[]{:S(2)}, u32[]{:S(2)}) collective-permute-start(bf16[256,1536]{1,0:T(8,128)(2,1)} %pad_maximum_fusion.3), channel_id=1, source_target_pairs={{0,1},{1,0},{2,3},{3,2},{4,5},{5,4},{6,7},{7,6},{8,9},{9,8},{10,11... | collective-permute-start | bytes 2359304 | tf_op jit(solution)/shard_map/ppermute | solution.py:265
  34.5 17.2 %collective-permute-start.3 = (bf16[2,2,320,256]{3,2,1,0:T(8,128)(2,1)S(1)}, bf16[2,2,320,256]{3,2,1,0:T(8,128)(2,1)S(1)}, u32[]{:S(2)}, u32[]{:S(2)}) collective-permute-start(bf16[2,2,320,256]{3,2,1,0:T(8,128)(2,1)S(1)} %pad_maximum_fusion.4.refs_4_), channel_id=1, source_target_pairs={{0,4},{2,6},{4,0},{6,2},{8,12},{10,14},{12,8},{14,10},{16,20},{18,... | collective-permute-start | bytes 1966088 | tf_op jit(solution)/shard_map/ppermute | solution.py:259
  36.1 24.1 %collective-permute-start.9 = (bf16[2,2,320,256]{3,2,1,0:T(8,128)(2,1)S(1)}, bf16[2,2,320,256]{3,2,1,0:T(8,128)(2,1)S(1)}, u32[]{:S(2)}, u32[]{:S(2)}) collective-permute-start(bf16[2,2,320,256]{3,2,1,0:T(8,128)(2,1)S(1)} %pad_maximum_fusion.4.refs_4_), channel_id=1, source_target_pairs={{0,2},{2,0},{4,6},{6,4},{8,10},{10,8},{12,14},{14,12},{16,18},{18,... | collective-permute-start | bytes 1966088 | tf_op jit(solution)/shard_map/ppermute | solution.py:259
  51.8 10.0 %collective-permute-start.10 = (bf16[2,2,320,256]{3,2,1,0:T(8,128)(2,1)S(1)}, bf16[2,2,320,256]{3,2,1,0:T(8,128)(2,1)S(1)}, u32[]{:S(2)}, u32[]{:S(2)}) collective-permute-start(bf16[2,2,320,256]{3,2,1,0:T(8,128)(2,1)S(1)} %pad_maximum_fusion.5.refs_5_), channel_id=1, source_target_pairs={{0,2},{2,0},{4,6},{6,4},{8,10},{10,8},{12,14},{14,12},{16,18},{18,... | collective-permute-start | bytes 1966088 | tf_op jit(solution)/shard_map/ppermute | solution.py:259
  51.9 28.7 %collective-permute-start.11 = (bf16[2,2,320,256]{3,2,1,0:T(8,128)(2,1)S(1)}, bf16[2,2,320,256]{3,2,1,0:T(8,128)(2,1)S(1)}, u32[]{:S(2)}, u32[]{:S(2)}) collective-permute-start(bf16[2,2,320,256]{3,2,1,0:T(8,128)(2,1)S(1)} %pad_maximum_fusion.5.refs_5_), channel_id=1, source_target_pairs={{0,4},{2,6},{4,0},{6,2},{8,12},{10,14},{12,8},{14,10},{16,20},{18,... | collective-permute-start | bytes 1966088 | tf_op jit(solution)/shard_map/ppermute | solution.py:259
  53.5 19.9 %collective-permute-start.6 = (bf16[3,336,128]{2,1,0:T(8,128)(2,1)S(1)}, bf16[3,336,128]{2,1,0:T(8,128)(2,1)S(1)}, u32[]{:S(2)}, u32[]{:S(2)}) collective-permute-start(bf16[3,336,128]{2,1,0:T(8,128)(2,1)S(1)} %pad_add_fusion.7), channel_id=1, source_target_pairs={{0,8},{2,10},{4,12},{6,14},{8,0},{10,2},{12,4},{14,6},{16,24},{18,... | collective-permute-start | bytes 774152 | tf_op jit(solution)/shard_map/ppermute | solution.py:259
  58.9 21.1 %collective-permute-start.7 = (bf16[3,336,128]{2,1,0:T(8,128)(2,1)S(1)}, bf16[3,336,128]{2,1,0:T(8,128)(2,1)S(1)}, u32[]{:S(2)}, u32[]{:S(2)}) collective-permute-start(bf16[3,336,128]{2,1,0:T(8,128)(2,1)S(1)} %get-tuple-element.63), channel_id=1, source_target_pairs={{0,16},{2,18},{4,20},{6,22},{8,24},{10,26},{12,28},{14,30},{16,0},... | collective-permute-start | bytes 774152 | tf_op jit(solution)/shard_map/ppermute | solution.py:259
  60.2 19.8 %collective-permute-start.8 = (bf16[3,336,128]{2,1,0:T(8,128)(2,1)S(1)}, bf16[3,336,128]{2,1,0:T(8,128)(2,1)S(1)}, u32[]{:S(2)}, u32[]{:S(2)}) collective-permute-start(bf16[3,336,128]{2,1,0:T(8,128)(2,1)S(1)} %get-tuple-element.64), channel_id=1, source_target_pairs={{0,24},{2,26},{4,28},{6,30},{8,16},{10,18},{12,20},{14,22},{16,8},... | collective-permute-start | bytes 774152 | tf_op jit(solution)/shard_map/ppermute | solution.py:259
  61.9 20.6 %collective-permute-start.12 = (bf16[2,2,320,256]{3,2,1,0:T(8,128)(2,1)S(1)}, bf16[2,2,320,256]{3,2,1,0:T(8,128)(2,1)S(1)}, u32[]{:S(2)}, u32[]{:S(2)}) collective-permute-start(bf16[2,2,320,256]{3,2,1,0:T(8,128)(2,1)S(1)} %collective-permute-done.3.refs_4_), channel_id=1, source_target_pairs={{0,2},{2,0},{4,6},{6,4},{8,10},{10,8},{12,14},{14,12},{16,18},{18,... | collective-permute-start | bytes 1966088 | tf_op jit(solution)/shard_map/ppermute | solution.py:259
  80.0 19.8 %collective-permute-start.14 = (bf16[2,2,320,128]{3,2,1,0:T(8,128)(2,1)S(1)}, bf16[2,2,320,128]{3,2,1,0:T(8,128)(2,1)S(1)}, u32[]{:S(2)}, u32[]{:S(2)}) collective-permute-start(bf16[2,2,320,128]{3,2,1,0:T(8,128)(2,1)S(1)} %pad_maximum_fusion.7.refs_4_), channel_id=1, source_target_pairs={{0,4},{2,6},{4,0},{6,2},{8,12},{10,14},{12,8},{14,10},{16,20},{18,... | collective-permute-start | bytes 983048 | tf_op jit(solution)/shard_map/ppermute | solution.py:259
  80.7 23.1 %collective-permute-start.15 = (bf16[2,2,320,128]{3,2,1,0:T(8,128)(2,1)S(1)}, bf16[2,2,320,128]{3,2,1,0:T(8,128)(2,1)}, u32[]{:S(2)}, u32[]{:S(2)}) collective-permute-start(bf16[2,2,320,128]{3,2,1,0:T(8,128)(2,1)S(1)} %pad_maximum_fusion.8.refs_5_), channel_id=1, source_target_pairs={{0,4},{2,6},{4,0},{6,2},{8,12},{10,14},{12,8},{14,10},{16,20},{18,... | collective-permute-start | bytes 983048 | tf_op jit(solution)/shard_map/ppermute | solution.py:259
  82.2 21.8 %collective-permute-start.21 = (bf16[2,2,320,128]{3,2,1,0:T(8,128)(2,1)S(1)}, bf16[2,2,320,128]{3,2,1,0:T(8,128)(2,1)S(1)}, u32[]{:S(2)}, u32[]{:S(2)}) collective-permute-start(bf16[2,2,320,128]{3,2,1,0:T(8,128)(2,1)S(1)} %pad_maximum_fusion.7.refs_4_), channel_id=1, source_target_pairs={{0,2},{2,0},{4,6},{6,4},{8,10},{10,8},{12,14},{14,12},{16,18},{18,... | collective-permute-start | bytes 983048 | tf_op jit(solution)/shard_map/ppermute | solution.py:259
  82.5 23.8 %collective-permute-start.22 = (bf16[2,2,320,128]{3,2,1,0:T(8,128)(2,1)S(1)}, bf16[2,2,320,128]{3,2,1,0:T(8,128)(2,1)S(1)}, u32[]{:S(2)}, u32[]{:S(2)}) collective-permute-start(bf16[2,2,320,128]{3,2,1,0:T(8,128)(2,1)S(1)} %pad_maximum_fusion.8.refs_5_), channel_id=1, source_target_pairs={{0,2},{2,0},{4,6},{6,4},{8,10},{10,8},{12,14},{14,12},{16,18},{18,... | collective-permute-start | bytes 983048 | tf_op jit(solution)/shard_map/ppermute | solution.py:259
  97.2 17.4 %collective-permute-start.20 = (bf16[320,256]{1,0:T(8,128)(2,1)S(1)}, bf16[320,256]{1,0:T(8,128)(2,1)S(1)}, u32[]{:S(2)}, u32[]{:S(2)}) collective-permute-start(bf16[320,256]{1,0:T(8,128)(2,1)S(1)} %get-tuple-element.77), channel_id=1, source_target_pairs={{0,24},{2,26},{4,28},{6,30},{8,16},{10,18},{12,20},{14,22},{16,8},... | collective-permute-start | bytes 491528 | tf_op jit(solution)/shard_map/ppermute | solution.py:259
  99.8 16.0 %collective-permute-start.19 = (bf16[320,256]{1,0:T(8,128)(2,1)S(1)}, bf16[320,256]{1,0:T(8,128)(2,1)S(1)}, u32[]{:S(2)}, u32[]{:S(2)}) collective-permute-start(bf16[320,256]{1,0:T(8,128)(2,1)S(1)} %get-tuple-element.76), channel_id=1, source_target_pairs={{0,16},{2,18},{4,20},{6,22},{8,24},{10,26},{12,28},{14,30},{16,0},... | collective-permute-start | bytes 491528 | tf_op jit(solution)/shard_map/ppermute | solution.py:259
  103.8 12.0 %collective-permute-start.18 = (bf16[320,256]{1,0:T(8,128)(2,1)S(1)}, bf16[320,256]{1,0:T(8,128)(2,1)S(1)}, u32[]{:S(2)}, u32[]{:S(2)}) collective-permute-start(bf16[320,256]{1,0:T(8,128)(2,1)S(1)} %get-tuple-element.75), channel_id=1, source_target_pairs={{0,8},{2,10},{4,12},{6,14},{8,0},{10,2},{12,4},{14,6},{16,24},{18,... | collective-permute-start | bytes 491528 | tf_op jit(solution)/shard_map/ppermute | solution.py:259
  104.0 15.5 %collective-permute-start.16 = (bf16[2,2,320,128]{3,2,1,0:T(8,128)(2,1)S(1)}, bf16[2,2,320,128]{3,2,1,0:T(8,128)(2,1)S(1)}, u32[]{:S(2)}, u32[]{:S(2)}) collective-permute-start(bf16[2,2,320,128]{3,2,1,0:T(8,128)(2,1)S(1)} %collective-permute-done.14.refs_4_), channel_id=1, source_target_pairs={{0,2},{2,0},{4,6},{6,4},{8,10},{10,8},{12,14},{14,12},{16,18},{18,... | collective-permute-start | bytes 983048 | tf_op jit(solution)/shard_map/ppermute | solution.py:259
  106.2 13.3 %collective-permute-start.17 = (bf16[2,2,320,128]{3,2,1,0:T(8,128)(2,1)}, bf16[2,2,320,128]{3,2,1,0:T(8,128)(2,1)S(1)}, u32[]{:S(2)}, u32[]{:S(2)}) collective-permute-start(bf16[2,2,320,128]{3,2,1,0:T(8,128)(2,1)} %collective-permute-done.15.refs_5_), channel_id=1, source_target_pairs={{0,2},{2,0},{4,6},{6,4},{8,10},{10,8},{12,14},{14,12},{16,18},{18,... | collective-permute-start | bytes 983048 | tf_op jit(solution)/shard_map/ppermute | solution.py:259
  118.0 24.8 %collective-permute-start.27 = (bf16[320,1536]{1,0:T(8,128)(2,1)}, bf16[320,1536]{1,0:T(8,128)(2,1)}, u32[]{:S(2)}, u32[]{:S(2)}) collective-permute-start(bf16[320,1536]{1,0:T(8,128)(2,1)} %convolution_convert_fusion), channel_id=1, source_target_pairs={{0,1},{1,0},{2,3},{3,2},{4,5},{5,4},{6,7},{7,6},{8,9},{9,8},{10,11... | collective-permute-start | bytes 2949128 | tf_op jit(solution)/shard_map/ppermute | solution.py:265
  129.4 7.7 %collective-permute-start.24 = (bf16[320,128]{1,0:T(8,128)(2,1)S(1)}, bf16[320,128]{1,0:T(8,128)(2,1)S(1)}, u32[]{:S(2)}, u32[]{:S(2)}) collective-permute-start(bf16[320,128]{1,0:T(8,128)(2,1)S(1)} %get-tuple-element.90), channel_id=1, source_target_pairs={{0,16},{2,18},{4,20},{6,22},{8,24},{10,26},{12,28},{14,30},{16,0},... | collective-permute-start | bytes 245768 | tf_op jit(solution)/shard_map/ppermute | solution.py:259
  139.8 9.9 %collective-permute-start.26 = (bf16[320,512]{1,0:T(8,128)(2,1)S(1)}, bf16[320,512]{1,0:T(8,128)(2,1)S(1)}, u32[]{:S(2)}, u32[]{:S(2)}) collective-permute-start(bf16[320,512]{1,0:T(8,128)(2,1)S(1)} %constant_dynamic-update-slice_fusion.2), channel_id=1, source_target_pairs={{0,1},{1,0},{2,3},{3,2},{4,5},{5,4},{6,7},{7,6},{8,9},{9,8},{10,11... | collective-permute-start | bytes 983048 | tf_op jit(solution)/shard_map/ppermute | solution.py:265
  (15 other events, 127.6 us)
